TPU v7x, 32 devices: a whole 2x2x4 slice. The times are simulated.
32 devices in a mesh: section: 8 (over z, core), dp: 4 (over y, x).
Axes of the slice: x: 2, y: 2, z: 4, core: 2. Of those that a mesh axis runs over, the one named last changes fastest.
Arguments:
- first_acts: bfloat16 [8, 512, 8192], P('section', 'dp'), may hold values from -6 to 6
- first_grads: bfloat16 [8, 512, 8192], P('section', 'dp'), may hold values from -6 to 6
- last_acts: bfloat16 [8, 512, 8192], P('section', 'dp'), may hold values from -6 to 6
- last_grads: bfloat16 [8, 512, 8192], P('section', 'dp'), may hold values from -6 to 6
- doc_lengths: int32 [4, 16], P('dp'), may hold values from 1 to 32, 128 in all within a row
- block_owner: int32 [16], replicated, may hold values from 0 to 3, as said below
Outputs:
- act_factor: float32 [8, 4, 8, 512, 512], P('section', 'dp')
- grad_factor: float32 [8, 4, 8, 512, 512], P('section', 'dp')
- act_cross: float32 [8, 4, 8, 512, 512], P('section', 'dp')
- grad_cross: float32 [8, 4, 8, 512, 512], P('section', 'dp')
Inputs may be any that keep to these rules, and one draw needn't show every extreme that they name: `doc_lengths`: documents fill their group's 128 rows exactly and the longest is exactly 32 rows. `block_owner`: one owner holds exactly 8 blocks, one holds none, every other holds exactly 4; which ones is drawn, except that the first and the last group always own blocks.
All inputs are finite; a program needn't handle non-finite values.
Results may differ from a plain program's by a relative error of at most 0.0037.
Values may be sent and summed in bfloat16 or wider, within the bound.
A program may use at most 320 MiB of HBM per device.

v0:
```python
import jax
import jax.numpy as jnp
from jax import lax
from jax.sharding import PartitionSpec as P


def shifted(block, axis, distance):
    devices = range(lax.axis_size(axis))
    route = [(i - distance, i) for i in devices if i - distance in devices]
    return lax.ppermute(block, axis, route)


def row_scale(doc_lengths, row_count, docs_all):
    doc_sizes = doc_lengths.astype(jnp.float32)
    doc_end = jnp.cumsum(doc_lengths)
    starts = doc_end - doc_lengths
    places = jnp.arange(row_count, dtype=jnp.int32)
    inside = (places[:, None] >= starts[None, :]) & (places[:, None] < doc_end[None, :])
    inverse = jnp.sum(jnp.where(inside, 1.0 / doc_sizes[None, :], jnp.float32(0.0)), axis=1)
    return jnp.sqrt(inverse / docs_all)


def slot_table(block_owner, groups, slot_count):
    blocks = block_owner.shape[0]
    position = jnp.arange(blocks, dtype=jnp.int32)
    same_owner = block_owner[:, None] == block_owner[None, :]
    earlier = position[None, :] < position[:, None]
    slot_index = jnp.sum(jnp.where(same_owner & earlier, 1, 0), axis=1).astype(jnp.int32)
    target = block_owner * slot_count + slot_index
    wanted = jnp.arange(groups * slot_count, dtype=jnp.int32)
    return jnp.where(wanted[:, None] == target[None, :], 1.0, 0.0).astype(jnp.bfloat16)


def into_slots(matrix, selector, groups, slot_count):
    row_count, widths = matrix.shape
    blocks = selector.shape[1]
    block_width = widths // blocks
    blocked = matrix.reshape(row_count, blocks, block_width)
    placed = jnp.einsum("cb,rbf->crf", selector, blocked, preferred_element_type=jnp.float32)
    return placed.astype(jnp.bfloat16).reshape(groups, slot_count, row_count, block_width)


def owner_gram(former, latter):
    return jnp.einsum("gkrf,gkrh->kfh", former, latter, preferred_element_type=jnp.float32)


def on_device(first_acts, first_grads, last_acts, last_grads, doc_lengths, block_owner):
    row_count = first_acts.shape[1]
    groups = lax.axis_size("dp")
    blocks = block_owner.shape[0]
    slot_count = 2 * blocks // groups
    row_weight = row_scale(doc_lengths[0], row_count, doc_lengths.shape[1] * groups)[:, None]

    def weighted(matrix):
        return (matrix[0].astype(jnp.float32) * row_weight).astype(jnp.bfloat16)

    own_acts = weighted(first_acts)
    own_grads = weighted(first_grads)
    tail_acts = weighted(last_acts)
    tail_grads = weighted(last_grads)
    selector = slot_table(block_owner, groups, slot_count)
    acts_in = lax.all_to_all(
        into_slots(own_acts, selector, groups, slot_count),
        "dp",
        split_axis=0,
        concat_axis=0,
        tiled=True,
    )
    grads_in = lax.all_to_all(
        into_slots(own_grads, selector, groups, slot_count),
        "dp",
        split_axis=0,
        concat_axis=0,
        tiled=True,
    )
    tail_in = lax.all_to_all(
        into_slots(tail_acts, selector, groups, slot_count),
        "dp",
        split_axis=0,
        concat_axis=0,
        tiled=True,
    )
    tail_grad_in = lax.all_to_all(
        into_slots(tail_grads, selector, groups, slot_count),
        "dp",
        split_axis=0,
        concat_axis=0,
        tiled=True,
    )
    prev_in, prev_grad_in = shifted((tail_in, tail_grad_in), "section", 1)
    first = owner_gram(acts_in, acts_in)
    second = owner_gram(grads_in, grads_in)
    third = owner_gram(prev_in, acts_in)
    fourth = owner_gram(prev_grad_in, grads_in)
    results = (first[None, None], second[None, None], third[None, None], fourth[None, None])
    return results


def solution(mesh):
    placed = (
        P("section", "dp", None),
        P("section", "dp", None),
        P("section", "dp", None),
        P("section", "dp", None),
        P("dp", None),
        P(),
    )
    return jax.shard_map(
        on_device,
        mesh=mesh,
        in_specs=placed,
        out_specs=(
            P("section", "dp", None, None, None),
            P("section", "dp", None, None, None),
            P("section", "dp", None, None, None),
            P("section", "dp", None, None, None),
        ),
        check_vma=False,
    )
```

profile of v0, /device:TPU:16, one launch (start us, length us, event | category | flops | bytes accessed | tf_op | source)
XLA Modules:
  0.0 262.6 jit_solution(10927848264889527164)
XLA Ops:
  0.6 0.0 copy-start
  0.6 1.0 select_reduce_fusion.1
  1.6 0.7 multiply_add_fusion
  2.3 0.7 divide_bitcast_fusion
  3.0 0.7 copy.37
  3.7 0.1 reduce
  3.9 0.7 fusion.33
  4.5 0.1 select_reduce_fusion
  4.6 2.4 copy.52
  7.1 0.0 copy-start.1
  7.1 0.0 copy-done
  7.1 0.8 copy.53
  7.9 0.0 copy-start.2
  7.9 0.7 copy-done.1
  8.7 0.8 copy.54
  9.5 0.2 copy-done.2
  9.7 0.8 copy.55
  10.5 5.4 %fusion = (bf16[128,16,512]{2,1,0:T(8,128)(2,1)S(1)}, bf16[128,16,512]{2,1,0:T(8,128)(2,1)S(1)}, bf16[128,16,512]{2,1,0:T(8,128)(2,1)}, bf16[128,16,512]{2,1,0:T(8,128)(2,1)}) fusion(f32[16,8,16,512]{3,2,1,0:T(8,128)S(1)} %copy.55, f32[128]{0:T(128)S(1)} %multiply_sqrt_fusion, f32[16,8,16,512]{3,2,1,0:T(8,128)S(1)} %copy.53, f32[16,8,16,512]{3,2,1,0:T(8,128)S(1)} %copy.54, ...), kind=kLoop, calls=%fused_computation.1 | loop fusion | flops 8388608 | bytes 25166336 | tf_op jit(solution)/shard_map/convert_element_type | solution.py:55
  15.9 3.4 %convert_bitcast_fusion = bf16[4,8,128,512]{3,1,0,2:T(8,128)(2,1)} fusion(bf16[128,16,512]{2,1,0:T(8,128)(2,1)S(1)} %get-tuple-element.4, s32[16]{0:T(128)S(1)} %multiply_add_fusion), kind=kOutput, calls=%fused_computation.12 | convolution fusion | flops 69207552 | bytes 6291520 | tf_op jit(solution)/shard_map/cb,rbf->crf/dot_general | solution.py:39
  19.3 7.9 %copy.45 = bf16[4,8,128,512]{2,3,1,0:T(8,128)(2,1)} copy(bf16[4,8,128,512]{3,1,0,2:T(8,128)(2,1)} %convert_bitcast_fusion) | data formatting | bytes 8388608 | tf_op jit(solution)/shard_map/reshape | solution.py:40
  27.1 4.8 %all-to-all-start.3 = ((bf16[4,8,128,512]{2,3,1,0:T(8,128)(2,1)}), bf16[4,8,128,512]{2,3,1,0:T(8,128)(2,1)}, u32[]{:S(2)}, u32[]{:S(2)}) async-start(bf16[4,8,128,512]{2,3,1,0:T(8,128)(2,1)} %copy.45), calls=%async_computation.3 | async-start | bytes 8388608 | tf_op jit(solution)/shard_map/all_to_all | solution.py:83
  32.0 4.9 %convert_bitcast_fusion.1 = bf16[4,8,128,512]{3,1,0,2:T(8,128)(2,1)} fusion(bf16[128,16,512]{2,1,0:T(8,128)(2,1)} %get-tuple-element.6, s32[16]{0:T(128)S(1)} %multiply_add_fusion), kind=kOutput, calls=%fused_computation.13 | convolution fusion | flops 69207552 | bytes 6291520 | tf_op jit(solution)/shard_map/cb,rbf->crf/dot_general | solution.py:39
  36.9 7.9 %copy.42 = bf16[4,8,128,512]{2,3,1,0:T(8,128)(2,1)} copy(bf16[4,8,128,512]{3,1,0,2:T(8,128)(2,1)} %convert_bitcast_fusion.1) | data formatting | bytes 8388608 | tf_op jit(solution)/shard_map/reshape | solution.py:40
  44.8 34.9 %all-to-all-done.3 = bf16[4,8,128,512]{2,3,1,0:T(8,128)(2,1)} async-done(((bf16[4,8,128,512]{2,3,1,0:T(8,128)(2,1)}), bf16[4,8,128,512]{2,3,1,0:T(8,128)(2,1)}, u32[]{:S(2)}, u32[]{:S(2)}) %all-to-all-start.3) | async-done | bytes 4194336 | tf_op jit(solution)/shard_map/all_to_all | solution.py:83
  79.7 5.1 %all-to-all-start.2 = ((bf16[4,8,128,512]{2,3,1,0:T(8,128)(2,1)}), bf16[4,8,128,512]{2,3,1,0:T(8,128)(2,1)}, u32[]{:S(2)}, u32[]{:S(2)}) async-start(bf16[4,8,128,512]{2,3,1,0:T(8,128)(2,1)} %copy.42), calls=%async_computation.2 | async-start | bytes 8388608 | tf_op jit(solution)/shard_map/all_to_all | solution.py:76
  84.8 2.9 %convert_bitcast_fusion.3 = bf16[4,8,128,512]{3,1,0,2:T(8,128)(2,1)S(1)} fusion(bf16[128,16,512]{2,1,0:T(8,128)(2,1)} %get-tuple-element.7, s32[16]{0:T(128)S(1)} %multiply_add_fusion), kind=kOutput, calls=%fused_computation.15 | convolution fusion | flops 69207552 | bytes 6291520 | tf_op jit(solution)/shard_map/cb,rbf->crf/dot_general | solution.py:39
  87.7 4.4 %copy.38 = bf16[4,8,128,512]{3,2,1,0:T(8,128)(2,1)} copy(bf16[4,8,128,512]{3,1,0,2:T(8,128)(2,1)S(1)} %convert_bitcast_fusion.3) | data formatting | bytes 8388608 | tf_op jit(solution)/shard_map/reshape | solution.py:40
  92.1 39.4 %all-to-all-done.2 = bf16[4,8,128,512]{2,3,1,0:T(8,128)(2,1)} async-done(((bf16[4,8,128,512]{2,3,1,0:T(8,128)(2,1)}), bf16[4,8,128,512]{2,3,1,0:T(8,128)(2,1)}, u32[]{:S(2)}, u32[]{:S(2)}) %all-to-all-start.2) | async-done | bytes 4194336 | tf_op jit(solution)/shard_map/all_to_all | solution.py:76
  131.5 4.8 %all-to-all-start = ((bf16[4,8,128,512]{3,2,1,0:T(8,128)(2,1)}), bf16[4,8,128,512]{3,2,1,0:T(8,128)(2,1)}, u32[]{:S(2)}, u32[]{:S(2)}) async-start(bf16[4,8,128,512]{3,2,1,0:T(8,128)(2,1)} %copy.38), calls=%async_computation | async-start | bytes 8388608 | tf_op jit(solution)/shard_map/all_to_all | solution.py:62
  136.3 4.6 %copy.43 = bf16[4,8,128,512]{2,3,0,1:T(8,128)(2,1)} copy(bf16[4,8,128,512]{2,3,1,0:T(8,128)(2,1)} %all-to-all-done.2) | data formatting | bytes 8388608 | tf_op jit(solution)/shard_map/all_to_all | solution.py:76
  140.9 1.9 collective-permute-start
  142.8 1.3 convert_bitcast_fusion.2
  144.2 4.4 %copy.40 = bf16[4,8,128,512]{3,2,1,0:T(8,128)(2,1)} copy(bf16[4,8,128,512]{3,1,0,2:T(8,128)(2,1)S(1)} %convert_bitcast_fusion.2) | data formatting | bytes 8388608 | tf_op jit(solution)/shard_map/reshape | solution.py:40
  148.6 34.6 %all-to-all-done = bf16[4,8,128,512]{3,2,1,0:T(8,128)(2,1)} async-done(((bf16[4,8,128,512]{3,2,1,0:T(8,128)(2,1)}), bf16[4,8,128,512]{3,2,1,0:T(8,128)(2,1)}, u32[]{:S(2)}, u32[]{:S(2)}) %all-to-all-start) | async-done | bytes 4194336 | tf_op jit(solution)/shard_map/all_to_all | solution.py:62
  183.2 4.9 %all-to-all-start.1 = ((bf16[4,8,128,512]{3,2,1,0:T(8,128)(2,1)}), bf16[4,8,128,512]{3,2,1,0:T(8,128)(2,1)}, u32[]{:S(2)}, u32[]{:S(2)}) async-start(bf16[4,8,128,512]{3,2,1,0:T(8,128)(2,1)} %copy.40), calls=%async_computation.1 | async-start | bytes 8388608 | tf_op jit(solution)/shard_map/all_to_all | solution.py:69
  188.1 4.7 %copy.46 = bf16[4,8,128,512]{2,3,0,1:T(8,128)(2,1)} copy(bf16[4,8,128,512]{2,3,1,0:T(8,128)(2,1)} %all-to-all-done.3) | data formatting | bytes 8388608 | tf_op jit(solution)/shard_map/all_to_all | solution.py:83
  192.8 2.1 collective-permute-start.1
  194.9 9.2 %convolution_bitcast_fusion.1 = f32[1,1,8,512,512]{4,3,2,1,0:T(8,128)} fusion(bf16[4,8,128,512]{3,2,1,0:T(8,128)(2,1)} %all-to-all-done), kind=kOutput, calls=%fused_computation.19 | convolution fusion | flops 2147483648 | bytes 12582912 | tf_op jit(solution)/shard_map/gkrf,gkrh->kfh/dot_general | solution.py:44
  204.2 30.8 %all-to-all-done.1 = bf16[4,8,128,512]{3,2,1,0:T(8,128)(2,1)} async-done(((bf16[4,8,128,512]{3,2,1,0:T(8,128)(2,1)}), bf16[4,8,128,512]{3,2,1,0:T(8,128)(2,1)}, u32[]{:S(2)}, u32[]{:S(2)}) %all-to-all-start.1) | async-done | bytes 4194336 | tf_op jit(solution)/shard_map/all_to_all | solution.py:69
  235.0 9.2 %convolution_bitcast_fusion = f32[1,1,8,512,512]{4,3,2,1,0:T(8,128)} fusion(bf16[4,8,128,512]{3,2,1,0:T(8,128)(2,1)} %all-to-all-done.1), kind=kOutput, calls=%fused_computation.18 | convolution fusion | flops 2147483648 | bytes 12582912 | tf_op jit(solution)/shard_map/gkrf,gkrh->kfh/dot_general | solution.py:44
  244.2 0.0 collective-permute-done
  244.2 9.2 %fusion.8 = f32[1,1,8,512,512]{4,3,2,1,0:T(8,128)} fusion(bf16[4,8,128,512]{2,3,0,1:T(8,128)(2,1)} %collective-permute-done, bf16[4,8,128,512]{3,2,1,0:T(8,128)(2,1)} %all-to-all-done), kind=kOutput, calls=%fused_computation.16 | convolution fusion | flops 2147483648 | bytes 16777216 | tf_op jit(solution)/shard_map/gkrf,gkrh->kfh/dot_general | solution.py:44
  253.4 0.0 collective-permute-done.1
  253.4 9.2 %fusion.11 = f32[1,1,8,512,512]{4,3,2,1,0:T(8,128)} fusion(bf16[4,8,128,512]{2,3,0,1:T(8,128)(2,1)} %collective-permute-done.1, bf16[4,8,128,512]{3,2,1,0:T(8,128)(2,1)} %all-to-all-done.1), kind=kOutput, calls=%fused_computation.17 | convolution fusion | flops 2147483648 | bytes 16777216 | tf_op jit(solution)/shard_map/gkrf,gkrh->kfh/dot_general | solution.py:44
  (2 shorter events, 0.0 us)
Async XLA Ops:
  0.6 6.4 %copy-start = (bf16[1,128,8192]{2,1,0:T(8,128)(2,1)S(1)}, bf16[1,128,8192]{2,1,0:T(8,128)(2,1)}, u32[]{:S(2)}) copy-start(bf16[1,128,8192]{2,1,0:T(8,128)(2,1)} %param.7) | copy-start | bytes 6291460
  7.1 1.6 copy-start.1
  7.9 1.8 copy-start.2
  27.1 52.5 %all-to-all-start.3 = ((bf16[4,8,128,512]{2,3,1,0:T(8,128)(2,1)}), bf16[4,8,128,512]{2,3,1,0:T(8,128)(2,1)}, u32[]{:S(2)}, u32[]{:S(2)}) async-start(bf16[4,8,128,512]{2,3,1,0:T(8,128)(2,1)} %copy.45), calls=%async_computation.3 | async-start | bytes 8388608 | tf_op jit(solution)/shard_map/all_to_all | solution.py:83
  79.7 51.8 %all-to-all-start.2 = ((bf16[4,8,128,512]{2,3,1,0:T(8,128)(2,1)}), bf16[4,8,128,512]{2,3,1,0:T(8,128)(2,1)}, u32[]{:S(2)}, u32[]{:S(2)}) async-start(bf16[4,8,128,512]{2,3,1,0:T(8,128)(2,1)} %copy.42), calls=%async_computation.2 | async-start | bytes 8388608 | tf_op jit(solution)/shard_map/all_to_all | solution.py:76
  131.5 51.7 %all-to-all-start = ((bf16[4,8,128,512]{3,2,1,0:T(8,128)(2,1)}), bf16[4,8,128,512]{3,2,1,0:T(8,128)(2,1)}, u32[]{:S(2)}, u32[]{:S(2)}) async-start(bf16[4,8,128,512]{3,2,1,0:T(8,128)(2,1)} %copy.38), calls=%async_computation | async-start | bytes 8388608 | tf_op jit(solution)/shard_map/all_to_all | solution.py:62
  140.9 103.3 %collective-permute-start = (bf16[4,8,128,512]{2,3,0,1:T(8,128)(2,1)}, bf16[4,8,128,512]{2,3,0,1:T(8,128)(2,1)}, u32[]{:S(2)}, u32[]{:S(2)}) collective-permute-start(bf16[4,8,128,512]{2,3,0,1:T(8,128)(2,1)} %copy.43), channel_id=1, source_target_pairs={{0,4},{4,8},{8,12},{12,16},{16,20},{20,24},{24,28},{1,5},{5,9},{9,... | collective-permute-start | bytes 12582920 | tf_op jit(solution)/shard_map/ppermute | solution.py:10
  183.2 51.8 %all-to-all-start.1 = ((bf16[4,8,128,512]{3,2,1,0:T(8,128)(2,1)}), bf16[4,8,128,512]{3,2,1,0:T(8,128)(2,1)}, u32[]{:S(2)}, u32[]{:S(2)}) async-start(bf16[4,8,128,512]{3,2,1,0:T(8,128)(2,1)} %copy.40), calls=%async_computation.1 | async-start | bytes 8388608 | tf_op jit(solution)/shard_map/all_to_all | solution.py:69
  192.8 60.7 %collective-permute-start.1 = (bf16[4,8,128,512]{2,3,0,1:T(8,128)(2,1)}, bf16[4,8,128,512]{2,3,0,1:T(8,128)(2,1)}, u32[]{:S(2)}, u32[]{:S(2)}) collective-permute-start(bf16[4,8,128,512]{2,3,0,1:T(8,128)(2,1)} %copy.46), channel_id=1, source_target_pairs={{0,4},{4,8},{8,12},{12,16},{16,20},{20,24},{24,28},{1,5},{5,9},{9,... | collective-permute-start | bytes 12582920 | tf_op jit(solution)/shard_map/ppermute | solution.py:10
where the time goes:
time: 265 us; the launch traced here: 263 us
  waiting for transfers between devices  140 us (53%)
  matrix products  49.5 us (19%)
  local copies, waits for them, and re-layouts  40.4 us (15%)
  starting transfers between devices  23.8 us (9%)
  other arithmetic  8.61 us (3%)
    all_to_all x1, waiting for transfers between devices, on_device(): lax.all_to_all(into_slots(tail_acts, selector, groups, slot_count), 'dp',...  39.4 us
    dot_general x4, matrix products, owner_gram(): jnp.einsum('gkrf,gkrh->kfh', former, latter, preferred_element_type=jnp.f...  36.9 us
    all_to_all x1, waiting for transfers between devices, on_device(): lax.all_to_all(into_slots(tail_grads, selector, groups, slot_count), 'dp'...  34.9 us
    all_to_all x1, waiting for transfers between devices, on_device(): lax.all_to_all(into_slots(own_acts, selector, groups, slot_count), 'dp',...  34.6 us
    all_to_all x1, waiting for transfers between devices, on_device(): lax.all_to_all(into_slots(own_grads, selector, groups, slot_count), 'dp',...  30.8 us
    reshape x4, local copies, waits for them, and re-layouts, into_slots(): placed.astype(jnp.bfloat16)  24.5 us
    dot_general x4, matrix products, into_slots(): jnp.einsum('cb,rbf->crf', selector, blocked, preferred_element_type=jnp.f...  12.6 us
    unnamed x10, local copies, waits for them, and re-layouts  5.86 us
  transfers between devices with their start and end apart: 6, of which 4 were waited for; matrix products, arithmetic and copies ran while one was open for 24% of the time, Pallas kernels for 0%

commit v1 on v0

--- a/solution.py
+++ b/solution.py
@@ -1,7 +1,322 @@
+import functools
+
 import jax
 import jax.numpy as jnp
 from jax import lax
+from jax.experimental import pallas as pl
+from jax.experimental.pallas import tpu as pltpu
 from jax.sharding import PartitionSpec as P
+
+MESH = pl.DeviceIdType.MESH
+
+ACROSS = {0: {1: 2, 2: 2}, 1: {1: 0, 2: 4}, 2: {1: 4, 2: 0}, 3: {1: 4, 2: 4}}
+
+
+def held_at(place):
+    return 8 if place == 0 else 4
+
+
+def base_of(place):
+    return 0 if place == 0 else 8 + 4 * (place - 1)
+
+
+def across_part(place, link):
+    return (0 if link == 1 else ACROSS[place][1]), ACROSS[place][link]
+
+
+def arrange_kernel(order_ref, lengths_ref, fa_ref, fg_ref, la_ref, lg_ref, first_ref, last_ref, weight):
+    docs = lengths_ref.shape[0]
+    rows = fa_ref.shape[1]
+
+    @pl.when(pl.program_id(0) == 0)
+    def _():
+        place = lax.broadcasted_iota(jnp.int32, (rows, 128), 0)
+        length = jnp.ones((rows, 128), jnp.int32)
+        start = jnp.int32(0)
+        for d in range(docs):
+            size = lengths_ref[d]
+            length = jnp.where((place >= start) & (place < start + size), size, length)
+            start = start + size
+        weight[...] = jnp.sqrt((1.0 / length.astype(jnp.float32)) / weight_docs(docs))
+
+    row_weight = weight[:, 0:1]
+    for half, ref in ((0, fa_ref), (1, fg_ref)):
+        first_ref[half, 0] = (ref[0].astype(jnp.float32) * row_weight).astype(jnp.bfloat16)
+    for half, ref in ((0, la_ref), (1, lg_ref)):
+        last_ref[half, 0] = (ref[0].astype(jnp.float32) * row_weight).astype(jnp.bfloat16)
+
+
+def weight_docs(docs):
+    return jnp.float32(docs * 4)
+
+
+def arrange(order, lengths, arrays, width):
+    rows = arrays[0].shape[1]
+    count = order.shape[0]
+    in_spec = pl.BlockSpec((1, rows, width), lambda i, order, lengths: (0, 0, order[i]))
+    out_spec = pl.BlockSpec((2, 1, rows, width), lambda i, order, lengths: (0, i, 0, 0))
+    shape = jax.ShapeDtypeStruct((2, count, rows, width), jnp.bfloat16)
+    return pl.pallas_call(
+        arrange_kernel,
+        grid_spec=pltpu.PrefetchScalarGridSpec(
+            num_scalar_prefetch=2,
+            grid=(count,),
+            in_specs=[in_spec] * 4,
+            out_specs=[out_spec] * 2,
+            scratch_shapes=[pltpu.VMEM((rows, 128), jnp.float32)],
+        ),
+        out_shape=(shape, shape),
+        compiler_params=pltpu.CompilerParams(vmem_limit_bytes=32 * 2**20),
+        name="arrange",
+    )(order, lengths, *arrays)
+
+
+def exchange_kernel(
+    most, sections, first, last, got_first, got_last, moved, relay, send_sem, recv_sem, move_send, move_recv
+):
+    me = lax.axis_index("dp")
+    section = lax.axis_index("section")
+    has_prev = section > 0
+    has_next = section < sections - 1
+
+    def move(half):
+        return pltpu.make_async_remote_copy(
+            src_ref=last.at[half],
+            dst_ref=moved.at[half],
+            send_sem=move_send.at[half],
+            recv_sem=move_recv.at[half],
+            device_id={"section": section + 1},
+            device_id_type=MESH,
+        )
+
+    def role(place):
+        def peer(link):
+            return {"dp": most ^ place ^ link}
+
+        def source(a):
+            return first.at[a] if a < 2 else moved.at[a - 2]
+
+        def target(a):
+            return got_first.at[a] if a < 2 else got_last.at[a - 2]
+
+        def copy(src, dst, a, sent, received, link):
+            return pltpu.make_async_remote_copy(
+                src_ref=src,
+                dst_ref=dst,
+                send_sem=send_sem.at[a, sent],
+                recv_sem=recv_sem.at[a, received],
+                device_id=peer(link),
+                device_id_type=MESH,
+            )
+
+        def direct(a, link):
+            to = place ^ link
+            n = held_at(to)
+            src = source(a).at[pl.ds(base_of(to), n)]
+            return copy(src, target(a).at[link - 1, pl.ds(0, n)], a, link - 1, link - 1, link)
+
+        def hop(a, link):
+            offset, n = across_part(place, link)
+            src = source(a).at[pl.ds(base_of(place ^ 3) + offset, n)]
+            return copy(src, relay.at[a, link - 1, pl.ds(0, n)], a, 1 + link, 1 + link, link)
+
+        def forward(a, link):
+            offset, n = across_part(place ^ link, link)
+            src = relay.at[a, link - 1, pl.ds(0, n)]
+            out = 3 - link
+            return copy(src, target(a).at[2, pl.ds(offset, n)], a, 3 + link, 3 + out, out)
+
+        def arrival(dst, a, received):
+            return copy(dst, dst, a, received, received, 1)
+
+        def wait_hop(a, link):
+            n = across_part(place ^ link, link)[1]
+            arrival(relay.at[a, link - 1, pl.ds(0, n)], a, 1 + link).wait_recv()
+
+        def sends(a):
+            return [link for link in (1, 2) if ACROSS[place][link]]
+
+        def relays(a):
+            return [link for link in (1, 2) if ACROSS[place ^ link][link]]
+
+        def start(a):
+            for link in sends(a):
+                hop(a, link).start()
+            for link in (1, 2):
+                direct(a, link).start()
+
+        def pass_on(a):
+            for link in relays(a):
+                wait_hop(a, link)
+                forward(a, link).start()
+
+        def finish(a):
+            n = held_at(place)
+            for link in (1, 2):
+                arrival(target(a).at[link - 1, pl.ds(0, n)], a, link - 1).wait_recv()
+            for out in (1, 2):
+                offset, n = across_part(place ^ 3, 3 - out)
+                if n:
+                    arrival(target(a).at[2, pl.ds(offset, n)], a, 3 + out).wait_recv()
+            for link in (1, 2):
+                direct(a, link).wait_send()
+            for link in sends(a):
+                hop(a, link).wait_send()
+            for link in relays(a):
+                forward(a, link).wait_send()
+
+        barrier = pltpu.get_barrier_semaphore()
+        for link in (1, 2):
+            pl.semaphore_signal(barrier, inc=1, device_id=peer(link), device_id_type=MESH)
+
+        @pl.when(has_next)
+        def _():
+            pl.semaphore_signal(barrier, inc=1, device_id={"section": section + 1}, device_id_type=MESH)
+
+        @pl.when(has_prev)
+        def _():
+            pl.semaphore_signal(barrier, inc=1, device_id={"section": section - 1}, device_id_type=MESH)
+
+        pl.semaphore_wait(barrier, 2 + has_prev.astype(jnp.int32) + has_next.astype(jnp.int32))
+
+        @pl.when(has_next)
+        def _():
+            for half in range(2):
+                move(half).start()
+
+        for a in range(2):
+            start(a)
+        for a in range(2):
+            pass_on(a)
+
+        @pl.when(has_prev)
+        def _():
+            for a in (2, 3):
+                move(a - 2).wait_recv()
+                start(a)
+            for a in (2, 3):
+                pass_on(a)
+
+        for a in range(2):
+            finish(a)
+
+        @pl.when(has_prev)
+        def _():
+            for a in (2, 3):
+                finish(a)
+
+        @pl.when(has_next)
+        def _():
+            for half in range(2):
+                move(half).wait_send()
+
+    for place in range(4):
+        pl.when(me == most ^ place)(functools.partial(role, place))
+
+
+def exchange(most, sections, first, last):
+    halves, count, rows, width = first.shape
+
+    def buffer(*lead):
+        return jax.ShapeDtypeStruct((*lead, rows, width), jnp.bfloat16)
+
+    hbm = pl.BlockSpec(memory_space=pl.ANY)
+    return pl.pallas_call(
+        functools.partial(exchange_kernel, most, sections),
+        in_specs=[hbm] * 2,
+        out_specs=[hbm] * 4,
+        out_shape=(buffer(2, 3, 8), buffer(2, 3, 8), buffer(2, count), buffer(4, 2, 4)),
+        scratch_shapes=[
+            pltpu.SemaphoreType.DMA((4, 6)),
+            pltpu.SemaphoreType.DMA((4, 6)),
+            pltpu.SemaphoreType.DMA((2,)),
+            pltpu.SemaphoreType.DMA((2,)),
+        ],
+        compiler_params=pltpu.CompilerParams(collective_id=most, has_side_effects=True),
+        name=f"exchange_{most}",
+    )(first, last)
+
+
+def gram_kernel(meta_ref, own_ref, got_ref, own_last_ref, got_last_ref, fa_ref, fg_ref, ca_ref, cg_ref):
+    filled = pl.program_id(0) < meta_ref[1]
+    has_prev = meta_ref[2] > 0
+    contract = (((0,), (0,)), ((), ()))
+
+    def joined(own, got, half):
+        return jnp.concatenate([own[half, 0], got[half, 0, 0], got[half, 1, 0], got[half, 2, 0]], axis=0)
+
+    for half, factor_ref, cross_ref in ((0, fa_ref, ca_ref), (1, fg_ref, cg_ref)):
+
+        @pl.when(filled)
+        def _():
+            latter = joined(own_ref, got_ref, half)
+            factor_ref[0, 0, 0] = lax.dot_general(latter, latter, contract, preferred_element_type=jnp.float32)
+
+        @pl.when(filled & has_prev)
+        def _():
+            latter = joined(own_ref, got_ref, half)
+            former = joined(own_last_ref, got_last_ref, half)
+            cross_ref[0, 0, 0] = lax.dot_general(former, latter, contract, preferred_element_type=jnp.float32)
+
+        @pl.when(jnp.logical_not(filled))
+        def _():
+            factor_ref[...] = jnp.zeros_like(factor_ref)
+
+        @pl.when(jnp.logical_not(filled & has_prev))
+        def _():
+            cross_ref[...] = jnp.zeros_like(cross_ref)
+
+
+def grams(meta, first, got_first, moved, got_last):
+    slots = got_first.shape[2]
+    rows, width = first.shape[2:]
+
+    def slot_of(i, meta):
+        return jnp.minimum(i, jnp.maximum(meta[1] - 1, 0))
+
+    own = pl.BlockSpec((2, 1, rows, width), lambda i, meta: (0, meta[0] + slot_of(i, meta), 0, 0))
+    got = pl.BlockSpec((2, 3, 1, rows, width), lambda i, meta: (0, 0, slot_of(i, meta), 0, 0))
+    out = pl.BlockSpec((1, 1, 1, width, width), lambda i, meta: (0, 0, i, 0, 0))
+    shape = jax.ShapeDtypeStruct((1, 1, slots, width, width), jnp.float32)
+    return pl.pallas_call(
+        gram_kernel,
+        grid_spec=pltpu.PrefetchScalarGridSpec(
+            num_scalar_prefetch=1, grid=(slots,), in_specs=[own, got, own, got], out_specs=[out] * 4
+        ),
+        out_shape=(shape,) * 4,
+        compiler_params=pltpu.CompilerParams(vmem_limit_bytes=40 * 2**20),
+        name="grams",
+    )(meta, first, got_first, moved, got_last)
+
+
+def on_square(first_acts, first_grads, last_acts, last_grads, doc_lengths, block_owner):
+    blocks = block_owner.shape[0]
+    sections = lax.axis_size("section")
+    me = lax.axis_index("dp").astype(jnp.int32)
+    position = jnp.arange(blocks, dtype=jnp.int32)
+    same_owner = block_owner[:, None] == block_owner[None, :]
+    slot_index = jnp.sum(jnp.where(same_owner & (position[None, :] < position[:, None]), 1, 0), axis=1)
+    owned = jnp.sum(jnp.where(block_owner[None, :] == jnp.arange(4)[:, None], 1, 0), axis=1).astype(jnp.int32)
+    most = jnp.sum(jnp.where(owned == 8, jnp.arange(4, dtype=jnp.int32), 0))
+    wanted_place = jnp.array([0] * 8 + [1] * 4 + [2] * 4 + [3] * 4, jnp.int32)
+    wanted_slot = jnp.array(list(range(8)) + list(range(4)) * 3, jnp.int32)
+    fits = ((block_owner ^ most)[None, :] == wanted_place[:, None]) & (slot_index[None, :] == wanted_slot[:, None])
+    order = jnp.sum(jnp.where(fits, position[None, :], 0), axis=1).astype(jnp.int32)
+    place = me ^ most
+    base = jnp.where(place == 0, 0, 4 + 4 * place)
+    mine = jnp.sum(jnp.where(block_owner == me, 1, 0))
+    meta = jnp.stack([base, mine, lax.axis_index("section")]).astype(jnp.int32)
+    width = first_acts.shape[2] // blocks
+    first, last = arrange(order, doc_lengths[0], (first_acts, first_grads, last_acts, last_grads), width)
+
+    def branch(which):
+        def run(meta, first, last):
+            got_first, got_last, moved, _ = exchange(which, sections, first, last)
+            return grams(meta, first, got_first, moved, got_last)
+
+        return run
+
+    return lax.switch(most, [branch(which) for which in range(4)], meta, first, last)
 
 
 def shifted(block, axis, distance):
@@ -106,7 +421,7 @@
         P(),
     )
     return jax.shard_map(
-        on_device,
+        on_square if mesh.shape["dp"] == 4 else on_device,
         mesh=mesh,
         in_specs=placed,
         out_specs=(

time: 265 us -> 191 us (0.72)
  Pallas kernels: 0 us -> 168 us
  waiting for transfers between devices: 140 us -> 0 us
  matrix products: 49.5 us -> 0 us
  local copies, waits for them, and re-layouts: 40.4 us -> 12.3 us
  starting transfers between devices: 23.8 us -> 0 us
  other arithmetic: 8.61 us -> 5.74 us
    pallas_call x0 -> x3, Pallas kernels: none -> 168 us  [the longest x1 140 us: exchange(): pl.pallas_call(functools.partial(exchange_kernel, most, sections), in_spe...]
    all_to_all x4 -> x0, waiting for transfers between devices: 140 us -> none  [the longest x1 39.4 us: on_device(): lax.all_to_all(into_slots(tail_acts, selector, groups, slot_count), 'dp',...]
    dot_general x8 -> x0, matrix products: 49.5 us -> none  [the longest x4 36.9 us: owner_gram(): jnp.einsum('gkrf,gkrh->kfh', former, latter, preferred_element_type=jnp.f...]
    reshape x5 -> x0, local copies, waits for them, and re-layouts: 25.3 us -> none  [the longest x4 24.5 us: into_slots(): placed.astype(jnp.bfloat16)]
    all_to_all x4 -> x0, starting transfers between devices: 19.7 us -> none  [the longest x1 5.1 us: on_device(): lax.all_to_all(into_slots(tail_acts, selector, groups, slot_count), 'dp',...]
    all_to_all x2 -> x0, local copies, waits for them, and re-layouts: 9.24 us -> none  [the longest x1 4.65 us: on_device(): lax.all_to_all(into_slots(tail_grads, selector, groups, slot_count), 'dp'...]
    convert_element_type x1 -> x0, other arithmetic: 5.37 us -> none  [weighted(): return (matrix[0].astype(jnp.float32) * row_weight).astype(jnp.bfloat16)]
    cond x0 -> x4, local copies, waits for them, and re-layouts: none -> 5.26 us
  transfers between devices with their start and end apart: 6 -> 0, of which waited for: 4 -> 0; matrix products, arithmetic and copies ran while one was open for 24% -> 0% of each run, Pallas kernels for 0% -> 0%
where the time goes in v1:
time: 191 us; the launch traced here: 188 us
  Pallas kernels  168 us (88%)
  local copies, waits for them, and re-layouts  12.3 us (6%)
  other arithmetic  5.74 us (3%)
  between operations  1.95 us (1%)
    pallas_call x1, Pallas kernels, exchange(): pl.pallas_call(functools.partial(exchange_kernel, most, sections), in_spe...  140 us
    pallas_call x1, Pallas kernels, grams(): pl.pallas_call(gram_kernel, grid_spec=pltpu.PrefetchScalarGridSpec(num_sc...  16.7 us
    pallas_call x1, Pallas kernels, arrange(): pl.pallas_call(arrange_kernel, grid_spec=pltpu.PrefetchScalarGridSpec(num...  11.2 us
    unnamed x10, local copies, waits for them, and re-layouts  7.01 us
    cond x4, local copies, waits for them, and re-layouts  5.26 us

profile of v1, /device:TPU:16, one launch (start us, length us, event | category | flops | bytes accessed | tf_op | source)
XLA Modules:
  0.0 187.5 jit_solution(3737297161604141045)
XLA Ops:
  0.6 0.8 select_reduce_fusion.2
  1.4 0.6 fusion.1
  3.3 1.9 %fusion.2 = (s32[]{:T(128)}, s32[16]{0:T(128)S(1)}) fusion(s32[16]{0:T(128)} %param.17, s32[]{:T(128)S(6)} %axis_index.22, s32[]{:T(128)} %fusion.1), kind=kLoop, calls=%fused_computation.9 | loop fusion | flops 63 | bytes 140 | tf_op jit(solution)/shard_map/reduce_sum | solution.py:307
  5.3 0.7 pad_add_fusion
  6.0 0.9 select_reduce_fusion.1
  6.9 0.8 select_reduce_fusion.order_ref
  7.7 0.0 copy-start.8
  7.7 1.6 copy-done.8
  9.3 0.0 copy-start.9
  9.3 1.6 copy-done.9
  10.9 0.0 copy-start.10
  10.9 1.6 copy-done.10
  12.5 0.0 copy-start.11
  12.5 1.6 copy-done.11
  14.0 0.0 copy-start.12
  14.1 0.7 copy-done.12
  14.7 11.2 %arrange.1 = (bf16[2,20,128,512]{3,2,1,0:T(8,128)(2,1)}, bf16[2,20,128,512]{3,2,1,0:T(8,128)(2,1)}) custom-call(s32[20]{0:T(128)S(1)} %select_reduce_fusion.order_ref, s32[16]{0:T(128)S(1)} %bitcast.4, bf16[1,128,8192]{2,1,0:T(8,128)(2,1)S(1)} %copy-done.8, bf16[1,128,8192]{2,1,0:T(8,128)(2,1)S(1)} %copy-done.9, bf16[1,128,8192]{2,1,0:T(8,128)(2,1)S(1)} %copy-done.10, ...), custom_call_target="tpu_custom_call" | custom-call | tf_op jit(solution)/shard_map/arrange/pallas_call | solution.py:59
  25.9 161.6 %conditional.1 = ((f32[1,1,8,512,512]{4,3,2,1,0:T(8,128)}, f32[1,1,8,512,512]{4,3,2,1,0:T(8,128)}, f32[1,1,8,512,512]{4,3,2,1,0:T(8,128)}, f32[1,1,8,512,512]{4,3,2,1,0:T(8,128)})) conditional(s32[]{:T(128)} %clamp.3, (bf16[2,20,128,512]{3,2,1,0:T(8,128)(2,1)}, bf16[2,20,128,512]{3,2,1,0:T(8,128)(2,1)}, ...), branch_computations={%region_5.6_spmd, %region_6.7_spmd, %region_7.8_spmd, %region_8.9_... | conditional | bytes 46137408 | solution.py:319
  25.9 139.6 %exchange_2.1 = (bf16[2,3,8,128,512]{4,3,2,1,0:T(8,128)(2,1)}, bf16[2,3,8,128,512]{4,3,2,1,0:T(8,128)(2,1)}, bf16[2,20,128,512]{3,2,1,0:T(8,128)(2,1)}, bf16[4,2,4,128,512]{4,3,2,1,0:T(8,128)(2,1)}) custom-call(bf16[2,20,128,512]{3,2,1,0:T(8,128)(2,1)} %get-tuple-element.37.first.own_ref, bf16[2,20,128,512]{3,2,1,0:T(8,128)(2,1)} %get-tuple-element.38.last), custom_call_target="tpu_custom_call" | custom-call | tf_op jit(solution)/shard_map/cond/branch_2_fun/exchange_2/pallas_call | solution.py:224
  165.6 0.0 copy-start.2
  165.6 2.8 %copy-done.2 = bf16[2,3,8,128,512]{4,3,2,1,0:T(8,128)(2,1)S(1)} copy-done((bf16[2,3,8,128,512]{4,3,2,1,0:T(8,128)(2,1)S(1)}, bf16[2,3,8,128,512]{4,3,2,1,0:T(8,128)(2,1)}, u32[]{:S(2)}) %copy-start.2) | copy-done | bytes 6291480 | tf_op jit(solution)/shard_map/cond
  168.3 0.0 copy-start.6
  168.3 2.5 %copy-done.6 = bf16[2,20,128,512]{3,2,1,0:T(8,128)(2,1)S(1)} copy-done((bf16[2,20,128,512]{3,2,1,0:T(8,128)(2,1)S(1)}, bf16[2,20,128,512]{3,2,1,0:T(8,128)(2,1)}, u32[]{:S(2)}) %copy-start.6) | copy-done | bytes 5242904 | tf_op jit(solution)/shard_map/cond
  170.8 16.7 %grams.6 = (f32[1,1,8,512,512]{4,3,2,1,0:T(8,128)}, f32[1,1,8,512,512]{4,3,2,1,0:T(8,128)}, f32[1,1,8,512,512]{4,3,2,1,0:T(8,128)}, f32[1,1,8,512,512]{4,3,2,1,0:T(8,128)}) custom-call(s32[3]{0:T(128)S(1)} %get-tuple-element.36.meta_ref, bf16[2,20,128,512]{3,2,1,0:T(8,128)(2,1)} %get-tuple-element.37.first.own_ref, ...), custom_call_target="tpu_custom_call" | custom-call | tf_op jit(solution)/shard_map/cond/branch_2_fun/grams/pallas_call | solution.py:281
Async XLA Ops:
  7.7 1.6 copy-start.8
  9.3 1.6 copy-start.9
  10.9 1.6 copy-start.10
  12.5 1.6 copy-start.11
  14.0 0.7 copy-start.12
  165.6 2.8 %copy-start.2 = (bf16[2,3,8,128,512]{4,3,2,1,0:T(8,128)(2,1)S(1)}, bf16[2,3,8,128,512]{4,3,2,1,0:T(8,128)(2,1)}, u32[]{:S(2)}) copy-start(bf16[2,3,8,128,512]{4,3,2,1,0:T(8,128)(2,1)} %get-tuple-element.39.got_ref) | copy-start | bytes 18874372 | tf_op jit(solution)/shard_map/cond
  168.3 2.5 %copy-start.6 = (bf16[2,20,128,512]{3,2,1,0:T(8,128)(2,1)S(1)}, bf16[2,20,128,512]{3,2,1,0:T(8,128)(2,1)}, u32[]{:S(2)}) copy-start(bf16[2,20,128,512]{3,2,1,0:T(8,128)(2,1)} %get-tuple-element.40.own_last_ref) | copy-start | bytes 15728644 | tf_op jit(solution)/shard_map/cond

commit v2 on v1

--- a/solution.py
+++ b/solution.py
@@ -8,6 +8,7 @@
 from jax.sharding import PartitionSpec as P
 
 MESH = pl.DeviceIdType.MESH
+GROUPS = 4
 
 ACROSS = {0: {1: 2, 2: 2}, 1: {1: 0, 2: 4}, 2: {1: 4, 2: 0}, 3: {1: 4, 2: 4}}
 
@@ -24,55 +25,119 @@
     return (0 if link == 1 else ACROSS[place][1]), ACROSS[place][link]
 
 
-def arrange_kernel(order_ref, lengths_ref, fa_ref, fg_ref, la_ref, lg_ref, first_ref, last_ref, weight):
+def arrange_kernel(
+    owner_ref,
+    lengths_ref,
+    fa_ref,
+    fg_ref,
+    la_ref,
+    lg_ref,
+    first_ref,
+    last_ref,
+    meta_ref,
+    weight,
+    staged,
+    sem,
+    place_of,
+    count,
+):
     docs = lengths_ref.shape[0]
+    blocks = owner_ref.shape[0]
     rows = fa_ref.shape[1]
-
-    @pl.when(pl.program_id(0) == 0)
+    width = first_ref.shape[3]
+    step = pl.program_id(0)
+    steps = pl.num_programs(0)
+
+    @pl.when(step == 0)
     def _():
-        place = lax.broadcasted_iota(jnp.int32, (rows, 128), 0)
+        row = lax.broadcasted_iota(jnp.int32, (rows, 128), 0)
         length = jnp.ones((rows, 128), jnp.int32)
         start = jnp.int32(0)
         for d in range(docs):
             size = lengths_ref[d]
-            length = jnp.where((place >= start) & (place < start + size), size, length)
+            length = jnp.where((row >= start) & (row < start + size), size, length)
             start = start + size
-        weight[...] = jnp.sqrt((1.0 / length.astype(jnp.float32)) / weight_docs(docs))
+        weight[...] = jnp.sqrt((1.0 / length.astype(jnp.float32)) / jnp.float32(docs * GROUPS))
+        for g in range(GROUPS):
+            count[g] = 0
+        for b in range(blocks):
+            owner = owner_ref[b]
+            place_of[b] = count[owner]
+            count[owner] = count[owner] + 1
+        most = jnp.int32(0)
+        for g in range(1, GROUPS):
+            most = jnp.where(count[g] == 8, jnp.int32(g), most)
+        for b in range(blocks):
+            place = owner_ref[b] ^ most
+            place_of[b] = place_of[b] + jnp.where(place == 0, 0, 4 + 4 * place)
+        me = lax.axis_index("dp")
+        place = me ^ most
+        meta_ref[0] = jnp.where(place == 0, 0, 4 + 4 * place)
+        meta_ref[1] = count[me]
+        meta_ref[2] = lax.axis_index("section")
+        meta_ref[3] = most
+
+    def outgoing(at, slot):
+        copies = []
+        for k in range(2):
+            to = place_of[2 * at + k]
+            for n, ref in enumerate((first_ref, first_ref, last_ref, last_ref)):
+                copies.append(pltpu.make_async_copy(staged.at[slot, k, n], ref.at[n % 2, to], sem.at[slot, k, n]))
+        return copies
+
+    slot = lax.rem(step, 2)
+
+    @pl.when(step >= 2)
+    def _():
+        for one in outgoing(step - 2, slot):
+            one.wait()
 
     row_weight = weight[:, 0:1]
-    for half, ref in ((0, fa_ref), (1, fg_ref)):
-        first_ref[half, 0] = (ref[0].astype(jnp.float32) * row_weight).astype(jnp.bfloat16)
-    for half, ref in ((0, la_ref), (1, lg_ref)):
-        last_ref[half, 0] = (ref[0].astype(jnp.float32) * row_weight).astype(jnp.bfloat16)
-
-
-def weight_docs(docs):
-    return jnp.float32(docs * 4)
-
-
-def arrange(order, lengths, arrays, width):
+    for k in range(2):
+        for n, ref in enumerate((fa_ref, fg_ref, la_ref, lg_ref)):
+            block = ref[0, :, k * width : (k + 1) * width].astype(jnp.float32)
+            staged[slot, k, n] = (block * row_weight).astype(jnp.bfloat16)
+    for one in outgoing(step, slot):
+        one.start()
+
+    @pl.when(step == steps - 1)
+    def _():
+        for one in outgoing(step - 1, 1 - slot):
+            one.wait()
+        for one in outgoing(step, slot):
+            one.wait()
+
+
+def arrange(owner, lengths, arrays):
     rows = arrays[0].shape[1]
-    count = order.shape[0]
-    in_spec = pl.BlockSpec((1, rows, width), lambda i, order, lengths: (0, 0, order[i]))
-    out_spec = pl.BlockSpec((2, 1, rows, width), lambda i, order, lengths: (0, i, 0, 0))
-    shape = jax.ShapeDtypeStruct((2, count, rows, width), jnp.bfloat16)
+    blocks = owner.shape[0]
+    width = arrays[0].shape[2] // blocks
+    in_spec = pl.BlockSpec((1, rows, 2 * width), lambda i, owner, lengths: (0, 0, i))
+    hbm = pl.BlockSpec(memory_space=pl.ANY)
+    shape = jax.ShapeDtypeStruct((2, 8 + 4 * (GROUPS - 1), rows, width), jnp.bfloat16)
     return pl.pallas_call(
         arrange_kernel,
         grid_spec=pltpu.PrefetchScalarGridSpec(
             num_scalar_prefetch=2,
-            grid=(count,),
+            grid=(blocks // 2,),
             in_specs=[in_spec] * 4,
-            out_specs=[out_spec] * 2,
-            scratch_shapes=[pltpu.VMEM((rows, 128), jnp.float32)],
+            out_specs=[hbm, hbm, pl.BlockSpec(memory_space=pltpu.SMEM)],
+            scratch_shapes=[
+                pltpu.VMEM((rows, 128), jnp.float32),
+                pltpu.VMEM((2, 2, 4, rows, width), jnp.bfloat16),
+                pltpu.SemaphoreType.DMA((2, 2, 4)),
+                pltpu.SMEM((blocks,), jnp.int32),
+                pltpu.SMEM((GROUPS,), jnp.int32),
+            ],
         ),
-        out_shape=(shape, shape),
-        compiler_params=pltpu.CompilerParams(vmem_limit_bytes=32 * 2**20),
+        out_shape=(shape, shape, jax.ShapeDtypeStruct((4,), jnp.int32)),
+        compiler_params=pltpu.CompilerParams(vmem_limit_bytes=60 * 2**20),
         name="arrange",
-    )(order, lengths, *arrays)
+    )(owner, lengths, *arrays)
 
 
 def exchange_kernel(
-    most, sections, first, last, got_first, got_last, moved, relay, send_sem, recv_sem, move_send, move_recv
+    most, sections, first, last, got, moved, relay, send_sem, recv_sem, move_send, move_recv
 ):
     me = lax.axis_index("dp")
     section = lax.axis_index("section")
@@ -97,7 +162,7 @@
             return first.at[a] if a < 2 else moved.at[a - 2]
 
         def target(a):
-            return got_first.at[a] if a < 2 else got_last.at[a - 2]
+            return got.at[a]
 
         def copy(src, dst, a, sent, received, link):
             return pltpu.make_async_remote_copy(
@@ -221,41 +286,42 @@
         return jax.ShapeDtypeStruct((*lead, rows, width), jnp.bfloat16)
 
     hbm = pl.BlockSpec(memory_space=pl.ANY)
+    apart = pl.BlockSpec(memory_space=pltpu.HBM)
     return pl.pallas_call(
         functools.partial(exchange_kernel, most, sections),
         in_specs=[hbm] * 2,
-        out_specs=[hbm] * 4,
-        out_shape=(buffer(2, 3, 8), buffer(2, 3, 8), buffer(2, count), buffer(4, 2, 4)),
+        out_specs=[hbm, apart, apart],
+        out_shape=(buffer(4, 3, 8), buffer(2, count), buffer(4, 2, 4)),
         scratch_shapes=[
             pltpu.SemaphoreType.DMA((4, 6)),
             pltpu.SemaphoreType.DMA((4, 6)),
             pltpu.SemaphoreType.DMA((2,)),
             pltpu.SemaphoreType.DMA((2,)),
         ],
-        compiler_params=pltpu.CompilerParams(collective_id=most, has_side_effects=True),
+        compiler_params=pltpu.CompilerParams(collective_id=most, has_side_effects=True, vmem_limit_bytes=60 * 2**20),
         name=f"exchange_{most}",
     )(first, last)
 
 
-def gram_kernel(meta_ref, own_ref, got_ref, own_last_ref, got_last_ref, fa_ref, fg_ref, ca_ref, cg_ref):
+def gram_kernel(meta_ref, own_ref, own_last_ref, got_ref, fa_ref, fg_ref, ca_ref, cg_ref):
     filled = pl.program_id(0) < meta_ref[1]
     has_prev = meta_ref[2] > 0
     contract = (((0,), (0,)), ((), ()))
 
-    def joined(own, got, half):
-        return jnp.concatenate([own[half, 0], got[half, 0, 0], got[half, 1, 0], got[half, 2, 0]], axis=0)
+    def joined(own, half, a):
+        return jnp.concatenate([own[half, 0], got_ref[a, 0, 0], got_ref[a, 1, 0], got_ref[a, 2, 0]], axis=0)
 
     for half, factor_ref, cross_ref in ((0, fa_ref, ca_ref), (1, fg_ref, cg_ref)):
 
         @pl.when(filled)
         def _():
-            latter = joined(own_ref, got_ref, half)
+            latter = joined(own_ref, half, half)
             factor_ref[0, 0, 0] = lax.dot_general(latter, latter, contract, preferred_element_type=jnp.float32)
 
         @pl.when(filled & has_prev)
         def _():
-            latter = joined(own_ref, got_ref, half)
-            former = joined(own_last_ref, got_last_ref, half)
+            latter = joined(own_ref, half, half)
+            former = joined(own_last_ref, half, 2 + half)
             cross_ref[0, 0, 0] = lax.dot_general(former, latter, contract, preferred_element_type=jnp.float32)
 
         @pl.when(jnp.logical_not(filled))
@@ -267,56 +333,41 @@
             cross_ref[...] = jnp.zeros_like(cross_ref)
 
 
-def grams(meta, first, got_first, moved, got_last):
-    slots = got_first.shape[2]
+def grams(meta, first, moved, got):
+    slots = got.shape[2]
     rows, width = first.shape[2:]
 
     def slot_of(i, meta):
         return jnp.minimum(i, jnp.maximum(meta[1] - 1, 0))
 
     own = pl.BlockSpec((2, 1, rows, width), lambda i, meta: (0, meta[0] + slot_of(i, meta), 0, 0))
-    got = pl.BlockSpec((2, 3, 1, rows, width), lambda i, meta: (0, 0, slot_of(i, meta), 0, 0))
+    arrived = pl.BlockSpec((4, 3, 1, rows, width), lambda i, meta: (0, 0, slot_of(i, meta), 0, 0))
     out = pl.BlockSpec((1, 1, 1, width, width), lambda i, meta: (0, 0, i, 0, 0))
     shape = jax.ShapeDtypeStruct((1, 1, slots, width, width), jnp.float32)
     return pl.pallas_call(
         gram_kernel,
         grid_spec=pltpu.PrefetchScalarGridSpec(
-            num_scalar_prefetch=1, grid=(slots,), in_specs=[own, got, own, got], out_specs=[out] * 4
+            num_scalar_prefetch=1, grid=(slots,), in_specs=[own, own, arrived], out_specs=[out] * 4
         ),
         out_shape=(shape,) * 4,
-        compiler_params=pltpu.CompilerParams(vmem_limit_bytes=40 * 2**20),
+        compiler_params=pltpu.CompilerParams(vmem_limit_bytes=60 * 2**20),
         name="grams",
-    )(meta, first, got_first, moved, got_last)
+    )(meta, first, moved, got)
 
 
 def on_square(first_acts, first_grads, last_acts, last_grads, doc_lengths, block_owner):
-    blocks = block_owner.shape[0]
     sections = lax.axis_size("section")
-    me = lax.axis_index("dp").astype(jnp.int32)
-    position = jnp.arange(blocks, dtype=jnp.int32)
-    same_owner = block_owner[:, None] == block_owner[None, :]
-    slot_index = jnp.sum(jnp.where(same_owner & (position[None, :] < position[:, None]), 1, 0), axis=1)
-    owned = jnp.sum(jnp.where(block_owner[None, :] == jnp.arange(4)[:, None], 1, 0), axis=1).astype(jnp.int32)
-    most = jnp.sum(jnp.where(owned == 8, jnp.arange(4, dtype=jnp.int32), 0))
-    wanted_place = jnp.array([0] * 8 + [1] * 4 + [2] * 4 + [3] * 4, jnp.int32)
-    wanted_slot = jnp.array(list(range(8)) + list(range(4)) * 3, jnp.int32)
-    fits = ((block_owner ^ most)[None, :] == wanted_place[:, None]) & (slot_index[None, :] == wanted_slot[:, None])
-    order = jnp.sum(jnp.where(fits, position[None, :], 0), axis=1).astype(jnp.int32)
-    place = me ^ most
-    base = jnp.where(place == 0, 0, 4 + 4 * place)
-    mine = jnp.sum(jnp.where(block_owner == me, 1, 0))
-    meta = jnp.stack([base, mine, lax.axis_index("section")]).astype(jnp.int32)
-    width = first_acts.shape[2] // blocks
-    first, last = arrange(order, doc_lengths[0], (first_acts, first_grads, last_acts, last_grads), width)
+    arrays = (first_acts, first_grads, last_acts, last_grads)
+    first, last, meta = arrange(block_owner, doc_lengths[0], arrays)
 
     def branch(which):
         def run(meta, first, last):
-            got_first, got_last, moved, _ = exchange(which, sections, first, last)
-            return grams(meta, first, got_first, moved, got_last)
+            got, moved, _ = exchange(which, sections, first, last)
+            return grams(meta, first, moved, got)
 
         return run
 
-    return lax.switch(most, [branch(which) for which in range(4)], meta, first, last)
+    return lax.switch(meta[3], [branch(which) for which in range(GROUPS)], meta, first, last)
 
 
 def shifted(block, axis, distance):
@@ -421,7 +472,7 @@
         P(),
     )
     return jax.shard_map(
-        on_square if mesh.shape["dp"] == 4 else on_device,
+        on_square if mesh.shape["dp"] == GROUPS else on_device,
         mesh=mesh,
         in_specs=placed,
         out_specs=(

time: 191 us -> 176 us (0.921); the launches traced: 188 us -> 176 us
  local copies, waits for them, and re-layouts: 12.3 us -> 0.58 us
  Pallas kernels: 168 us -> 174 us
  other arithmetic: 5.74 us -> 0 us
    unnamed x10 -> x0, local copies, waits for them, and re-layouts: 7.01 us -> none
    pallas_call x1, Pallas kernels: 16.7 us -> 23.4 us  [grams(): pl.pallas_call(gram_kernel, grid_spec=pltpu.PrefetchScalarGridSpec(num_sc...]
    cond x4 -> x0, local copies, waits for them, and re-layouts: 5.26 us -> none
    reduce_sum x5 -> x0, other arithmetic: 5.02 us -> none  [the longest x1 1.94 us: on_square(): mine = jnp.sum(jnp.where(block_owner == me, 1, 0))]
where the time goes in v2:
time: 176 us
  Pallas kernels  174 us (99%)
    pallas_call x1, Pallas kernels, exchange(): pl.pallas_call(functools.partial(exchange_kernel, most, sections), in_spe...  140 us
    pallas_call x1, Pallas kernels, grams(): pl.pallas_call(gram_kernel, grid_spec=pltpu.PrefetchScalarGridSpec(num_sc...  23.4 us
    pallas_call x1, Pallas kernels, arrange(): pl.pallas_call(arrange_kernel, grid_spec=pltpu.PrefetchScalarGridSpec(num...  11.1 us

profile of v2, /device:TPU:16, one launch (start us, length us, event | category | flops | bytes accessed | tf_op | source)
XLA Modules:
  0.0 176.1 jit_solution(6308636181971410904)
XLA Ops:
  0.6 11.1 %arrange.1 = (bf16[2,20,128,512]{3,2,1,0:T(8,128)(2,1)}, bf16[2,20,128,512]{3,2,1,0:T(8,128)(2,1)}, s32[4]{0:T(128)S(1)}) custom-call(s32[16]{0:T(128)} %owner_ref.1, s32[16]{0:T(128)} %bitcast.2, bf16[1,128,8192]{2,1,0:T(8,128)(2,1)} %fa_ref.1, bf16[1,128,8192]{2,1,0:T(8,128)(2,1)} %fg_ref.1, bf16[1,128,8192]{2,1,0:T(8,128)(2,1)} %la_ref.1, ...), custom_call_target="tpu_custom_call" | custom-call | tf_op jit(solution)/shard_map/arrange/pallas_call | solution.py:118
  11.7 0.6 slice.3
  13.0 163.2 %conditional.1 = ((f32[1,1,8,512,512]{4,3,2,1,0:T(8,128)}, f32[1,1,8,512,512]{4,3,2,1,0:T(8,128)}, f32[1,1,8,512,512]{4,3,2,1,0:T(8,128)}, f32[1,1,8,512,512]{4,3,2,1,0:T(8,128)})) conditional(s32[]{:T(128)} %bitcast.1, (bf16[2,20,128,512]{3,2,1,0:T(8,128)(2,1)}, bf16[2,20,128,512]{3,2,1,0:T(8,128)(2,1)}, ...), branch_computations={%region_0.0_spmd, %region_1.0_spmd, %region_2.0_spmd, %region_3.0_... | conditional | bytes 8 | solution.py:370
  13.0 139.7 %exchange_0.1 = (bf16[4,3,8,128,512]{4,3,2,1,0:T(8,128)(2,1)}, bf16[2,20,128,512]{3,2,1,0:T(8,128)(2,1)}, bf16[4,2,4,128,512]{4,3,2,1,0:T(8,128)(2,1)}) custom-call(bf16[2,20,128,512]{3,2,1,0:T(8,128)(2,1)} %get-tuple-element.25.first.own_ref, bf16[2,20,128,512]{3,2,1,0:T(8,128)(2,1)} %get-tuple-element.26.last), custom_call_target="tpu_custom_call" | custom-call | tf_op jit(solution)/shard_map/cond/branch_0_fun/exchange_0/pallas_call | solution.py:290
  152.7 23.4 %grams.4 = (f32[1,1,8,512,512]{4,3,2,1,0:T(8,128)}, f32[1,1,8,512,512]{4,3,2,1,0:T(8,128)}, f32[1,1,8,512,512]{4,3,2,1,0:T(8,128)}, f32[1,1,8,512,512]{4,3,2,1,0:T(8,128)}) custom-call(s32[4]{0:T(128)S(1)} %get-tuple-element.24.meta_ref, bf16[2,20,128,512]{3,2,1,0:T(8,128)(2,1)} %get-tuple-element.25.first.own_ref, ...), custom_call_target="tpu_custom_call" | custom-call | tf_op jit(solution)/shard_map/cond/branch_0_fun/grams/pallas_call | solution.py:347

commit v3 on v2

--- a/solution.py
+++ b/solution.py
@@ -11,6 +11,8 @@
 GROUPS = 4
 
 ACROSS = {0: {1: 2, 2: 2}, 1: {1: 0, 2: 4}, 2: {1: 4, 2: 0}, 3: {1: 4, 2: 4}}
+ACROSS_QUARTER = {0: {1: 1, 2: 0}, 1: {1: 0, 2: 1}, 2: {1: 1, 2: 0}, 3: {1: 1, 2: 1}}
+QUARTERS = 4
 
 
 def held_at(place):
@@ -19,10 +21,6 @@
 
 def base_of(place):
     return 0 if place == 0 else 8 + 4 * (place - 1)
-
-
-def across_part(place, link):
-    return (0 if link == 1 else ACROSS[place][1]), ACROSS[place][link]
 
 
 def arrange_kernel(
@@ -92,7 +90,7 @@
         for one in outgoing(step - 2, slot):
             one.wait()
 
-    row_weight = weight[:, 0:1]
+    row_weight = jnp.concatenate([weight[...]] * (width // 128), axis=1)
     for k in range(2):
         for n, ref in enumerate((fa_ref, fg_ref, la_ref, lg_ref)):
             block = ref[0, :, k * width : (k + 1) * width].astype(jnp.float32)
@@ -137,12 +135,31 @@
 
 
 def exchange_kernel(
-    most, sections, first, last, got, moved, relay, send_sem, recv_sem, move_send, move_recv
+    most,
+    sections,
+    first,
+    last,
+    got,
+    moved,
+    early,
+    relay,
+    relay_quarter,
+    send_sem,
+    recv_sem,
+    move_send,
+    move_recv,
+    on_send,
+    on_recv,
 ):
     me = lax.axis_index("dp")
     section = lax.axis_index("section")
+    plane = section // 2
+    core = section - 2 * plane
     has_prev = section > 0
     has_next = section < sections - 1
+    planes = sections // 2
+    leaving = jnp.where(core == 1, planes - 1 - plane, 0)
+    entering = jnp.where((core == 0) & has_prev, planes - plane, 0)
 
     def move(half):
         return pltpu.make_async_remote_copy(
@@ -158,77 +175,116 @@
         def peer(link):
             return {"dp": most ^ place ^ link}
 
-        def source(a):
-            return first.at[a] if a < 2 else moved.at[a - 2]
-
-        def target(a):
-            return got.at[a]
-
-        def copy(src, dst, a, sent, received, link):
+        def go_on(half, quarter):
+            m = held_at(place) // QUARTERS
+            span = pl.ds(quarter * m, m)
+            at = half * QUARTERS + quarter
             return pltpu.make_async_remote_copy(
-                src_ref=src,
-                dst_ref=dst,
-                send_sem=send_sem.at[a, sent],
-                recv_sem=recv_sem.at[a, received],
-                device_id=peer(link),
+                src_ref=early.at[half, :, span],
+                dst_ref=got.at[2 + half, :, span],
+                send_sem=on_send.at[at],
+                recv_sem=on_recv.at[at],
+                device_id={"section": section + 1},
                 device_id_type=MESH,
             )
 
-        def direct(a, link):
-            to = place ^ link
-            n = held_at(to)
-            src = source(a).at[pl.ds(base_of(to), n)]
-            return copy(src, target(a).at[link - 1, pl.ds(0, n)], a, link - 1, link - 1, link)
-
-        def hop(a, link):
-            offset, n = across_part(place, link)
-            src = source(a).at[pl.ds(base_of(place ^ 3) + offset, n)]
-            return copy(src, relay.at[a, link - 1, pl.ds(0, n)], a, 1 + link, 1 + link, link)
-
-        def forward(a, link):
-            offset, n = across_part(place ^ link, link)
-            src = relay.at[a, link - 1, pl.ds(0, n)]
-            out = 3 - link
-            return copy(src, target(a).at[2, pl.ds(offset, n)], a, 3 + link, 3 + out, out)
-
-        def arrival(dst, a, received):
-            return copy(dst, dst, a, received, received, 1)
-
-        def wait_hop(a, link):
-            n = across_part(place ^ link, link)[1]
-            arrival(relay.at[a, link - 1, pl.ds(0, n)], a, 1 + link).wait_recv()
-
-        def sends(a):
-            return [link for link in (1, 2) if ACROSS[place][link]]
-
-        def relays(a):
-            return [link for link in (1, 2) if ACROSS[place ^ link][link]]
-
-        def start(a):
-            for link in sends(a):
-                hop(a, link).start()
-            for link in (1, 2):
-                direct(a, link).start()
-
-        def pass_on(a):
-            for link in relays(a):
-                wait_hop(a, link)
-                forward(a, link).start()
-
-        def finish(a):
-            n = held_at(place)
-            for link in (1, 2):
-                arrival(target(a).at[link - 1, pl.ds(0, n)], a, link - 1).wait_recv()
-            for out in (1, 2):
-                offset, n = across_part(place ^ 3, 3 - out)
-                if n:
-                    arrival(target(a).at[2, pl.ds(offset, n)], a, 3 + out).wait_recv()
-            for link in (1, 2):
-                direct(a, link).wait_send()
-            for link in sends(a):
-                hop(a, link).wait_send()
-            for link in relays(a):
-                forward(a, link).wait_send()
+        class Part:
+            def __init__(self, source, target, sem, relay_ref, quarter=None):
+                self.source, self.target, self.sem, self.relay = source, target, sem, relay_ref
+                self.quarter = quarter
+                self.across = ACROSS if quarter is None else ACROSS_QUARTER
+                self.sends = [link for link in (1, 2) if self.across[place][link]]
+                self.relays = [link for link in (1, 2) if self.across[place ^ link][link]]
+
+            def span(self, to, offset, n, base=0):
+                if self.quarter is not None:
+                    offset = offset + self.quarter * (held_at(to) // QUARTERS)
+                return pl.ds(base + offset, n)
+
+            def size(self, to):
+                return held_at(to) if self.quarter is None else held_at(to) // QUARTERS
+
+            def part(self, source_place, link):
+                return (0 if link == 1 else self.across[source_place][1]), self.across[source_place][link]
+
+            def copy(self, src, dst, sent, received, link):
+                return pltpu.make_async_remote_copy(
+                    src_ref=src,
+                    dst_ref=dst,
+                    send_sem=send_sem.at[self.sem, sent],
+                    recv_sem=recv_sem.at[self.sem, received],
+                    device_id=peer(link),
+                    device_id_type=MESH,
+                )
+
+            def direct(self, link):
+                to = place ^ link
+                n = self.size(to)
+                src = self.source.at[self.span(to, 0, n, base_of(to))]
+                return self.copy(src, self.target.at[link - 1, self.span(to, 0, n)], link - 1, link - 1, link)
+
+            def hop(self, link):
+                offset, n = self.part(place, link)
+                to = place ^ 3
+                src = self.source.at[self.span(to, offset, n, base_of(to))]
+                return self.copy(src, self.relay.at[link - 1, pl.ds(0, n)], 1 + link, 1 + link, link)
+
+            def forward(self, link):
+                offset, n = self.part(place ^ link, link)
+                out = 3 - link
+                to = place ^ out
+                dst = self.target.at[2, self.span(to, offset, n)]
+                return self.copy(self.relay.at[link - 1, pl.ds(0, n)], dst, 3 + link, 3 + out, out)
+
+            def arrival(self, dst, received):
+                return self.copy(dst, dst, received, received, 1)
+
+            def start(self):
+                for link in self.sends:
+                    self.hop(link).start()
+                for link in (1, 2):
+                    self.direct(link).start()
+
+            def pass_on(self):
+                for link in self.relays:
+                    n = self.part(place ^ link, link)[1]
+                    self.arrival(self.relay.at[link - 1, pl.ds(0, n)], 1 + link).wait_recv()
+                    self.forward(link).start()
+
+            def wait_arrivals(self):
+                n = self.size(place)
+                for link in (1, 2):
+                    self.arrival(self.target.at[link - 1, self.span(place, 0, n)], link - 1).wait_recv()
+                for out in (1, 2):
+                    offset, n = self.part(place ^ 3, 3 - out)
+                    if n:
+                        self.arrival(self.target.at[2, self.span(place, offset, n)], 3 + out).wait_recv()
+
+            def wait_sent(self):
+                for link in (1, 2):
+                    self.direct(link).wait_send()
+                for link in self.sends:
+                    self.hop(link).wait_send()
+                for link in self.relays:
+                    self.forward(link).wait_send()
+
+        def whole(half):
+            return Part(first.at[half], got.at[half], half, relay.at[half])
+
+        def late(half, quarter):
+            at = half * QUARTERS + quarter
+            return Part(moved.at[half], got.at[2 + half], 2 + at, relay_quarter.at[at], quarter)
+
+        def ahead(half, quarter):
+            at = (2 + half) * QUARTERS + quarter
+            return Part(last.at[half], early.at[half], 2 + at, relay_quarter.at[at], quarter)
+
+        def each(low, high, act):
+            for half in range(2):
+
+                @pl.loop(low, high)
+                def _(quarter):
+                    act(half, quarter)
 
         barrier = pltpu.get_barrier_semaphore()
         for link in (1, 2):
@@ -249,26 +305,38 @@
             for half in range(2):
                 move(half).start()
 
-        for a in range(2):
-            start(a)
-        for a in range(2):
-            pass_on(a)
+        for half in range(2):
+            whole(half).start()
+        each(0, leaving, lambda half, quarter: ahead(half, quarter).start())
+        for half in range(2):
+            whole(half).pass_on()
+        each(0, leaving, lambda half, quarter: ahead(half, quarter).pass_on())
+
+        late_from = jnp.where(has_prev, entering, QUARTERS)
 
         @pl.when(has_prev)
         def _():
-            for a in (2, 3):
-                move(a - 2).wait_recv()
-                start(a)
-            for a in (2, 3):
-                pass_on(a)
-
-        for a in range(2):
-            finish(a)
-
-        @pl.when(has_prev)
-        def _():
-            for a in (2, 3):
-                finish(a)
+            for half in range(2):
+                move(half).wait_recv()
+
+        each(late_from, QUARTERS, lambda half, quarter: late(half, quarter).start())
+
+        def send_on(half, quarter):
+            ahead(half, quarter).wait_arrivals()
+            go_on(half, quarter).start()
+
+        each(0, leaving, send_on)
+        each(late_from, QUARTERS, lambda half, quarter: late(half, quarter).pass_on())
+
+        for half in range(2):
+            whole(half).wait_arrivals()
+        each(late_from, QUARTERS, lambda half, quarter: late(half, quarter).wait_arrivals())
+        each(0, entering, lambda half, quarter: go_on(half, quarter).wait_recv())
+        for half in range(2):
+            whole(half).wait_sent()
+        each(0, leaving, lambda half, quarter: ahead(half, quarter).wait_sent())
+        each(0, leaving, lambda half, quarter: go_on(half, quarter).wait_send())
+        each(late_from, QUARTERS, lambda half, quarter: late(half, quarter).wait_sent())
 
         @pl.when(has_next)
         def _():
@@ -286,49 +354,59 @@
         return jax.ShapeDtypeStruct((*lead, rows, width), jnp.bfloat16)
 
     hbm = pl.BlockSpec(memory_space=pl.ANY)
-    apart = pl.BlockSpec(memory_space=pltpu.HBM)
     return pl.pallas_call(
         functools.partial(exchange_kernel, most, sections),
         in_specs=[hbm] * 2,
-        out_specs=[hbm, apart, apart],
-        out_shape=(buffer(4, 3, 8), buffer(2, count), buffer(4, 2, 4)),
+        out_specs=[hbm] * 5,
+        out_shape=(
+            buffer(4, 3, 8),
+            buffer(2, count),
+            buffer(2, 3, 8),
+            buffer(2, 2, 4),
+            buffer(4 * QUARTERS, 2, 1),
+        ),
         scratch_shapes=[
-            pltpu.SemaphoreType.DMA((4, 6)),
-            pltpu.SemaphoreType.DMA((4, 6)),
+            pltpu.SemaphoreType.DMA((2 + 4 * QUARTERS, 6)),
+            pltpu.SemaphoreType.DMA((2 + 4 * QUARTERS, 6)),
             pltpu.SemaphoreType.DMA((2,)),
             pltpu.SemaphoreType.DMA((2,)),
+            pltpu.SemaphoreType.DMA((2 * QUARTERS,)),
+            pltpu.SemaphoreType.DMA((2 * QUARTERS,)),
         ],
-        compiler_params=pltpu.CompilerParams(collective_id=most, has_side_effects=True, vmem_limit_bytes=60 * 2**20),
+        compiler_params=pltpu.CompilerParams(
+            collective_id=most, has_side_effects=True, vmem_limit_bytes=60 * 2**20
+        ),
         name=f"exchange_{most}",
     )(first, last)
 
 
-def gram_kernel(meta_ref, own_ref, own_last_ref, got_ref, fa_ref, fg_ref, ca_ref, cg_ref):
-    filled = pl.program_id(0) < meta_ref[1]
-    has_prev = meta_ref[2] > 0
+def gram_kernel(meta_ref, own_ref, own_last_ref, got_ref, got_last_ref, fa_ref, fg_ref, ca_ref, cg_ref):
+    side = pl.program_id(0)
+    filled = pl.program_id(1) < meta_ref[1]
+    crossed = filled & (meta_ref[2] > 0)
     contract = (((0,), (0,)), ((), ()))
 
-    def joined(own, half, a):
-        return jnp.concatenate([own[half, 0], got_ref[a, 0, 0], got_ref[a, 1, 0], got_ref[a, 2, 0]], axis=0)
+    def joined(own, got):
+        return jnp.concatenate([own[0, 0], got[0, 0, 0], got[0, 1, 0], got[0, 2, 0]], axis=0)
 
     for half, factor_ref, cross_ref in ((0, fa_ref, ca_ref), (1, fg_ref, cg_ref)):
 
-        @pl.when(filled)
-        def _():
-            latter = joined(own_ref, half, half)
+        @pl.when((side == half) & filled)
+        def _():
+            latter = joined(own_ref, got_ref)
             factor_ref[0, 0, 0] = lax.dot_general(latter, latter, contract, preferred_element_type=jnp.float32)
 
-        @pl.when(filled & has_prev)
-        def _():
-            latter = joined(own_ref, half, half)
-            former = joined(own_last_ref, half, 2 + half)
+        @pl.when((side == half) & crossed)
+        def _():
+            latter = joined(own_ref, got_ref)
+            former = joined(own_last_ref, got_last_ref)
             cross_ref[0, 0, 0] = lax.dot_general(former, latter, contract, preferred_element_type=jnp.float32)
 
-        @pl.when(jnp.logical_not(filled))
+        @pl.when((side == half) & jnp.logical_not(filled))
         def _():
             factor_ref[...] = jnp.zeros_like(factor_ref)
 
-        @pl.when(jnp.logical_not(filled & has_prev))
+        @pl.when((side == half) & jnp.logical_not(crossed))
         def _():
             cross_ref[...] = jnp.zeros_like(cross_ref)
 
@@ -340,19 +418,26 @@
     def slot_of(i, meta):
         return jnp.minimum(i, jnp.maximum(meta[1] - 1, 0))
 
-    own = pl.BlockSpec((2, 1, rows, width), lambda i, meta: (0, meta[0] + slot_of(i, meta), 0, 0))
-    arrived = pl.BlockSpec((4, 3, 1, rows, width), lambda i, meta: (0, 0, slot_of(i, meta), 0, 0))
-    out = pl.BlockSpec((1, 1, 1, width, width), lambda i, meta: (0, 0, i, 0, 0))
+    def arrived(skip):
+        return pl.BlockSpec((1, 3, 1, rows, width), lambda h, i, meta: (skip + h, 0, slot_of(i, meta), 0, 0))
+
+    own = pl.BlockSpec((1, 1, rows, width), lambda h, i, meta: (h, meta[0] + slot_of(i, meta), 0, 0))
+    block = (1, 1, 1, width, width)
+    acts = pl.BlockSpec(block, lambda h, i, meta: (0, 0, jnp.where(h == 0, i, slots - 1), 0, 0))
+    grads = pl.BlockSpec(block, lambda h, i, meta: (0, 0, jnp.where(h == 0, 0, i), 0, 0))
     shape = jax.ShapeDtypeStruct((1, 1, slots, width, width), jnp.float32)
     return pl.pallas_call(
         gram_kernel,
         grid_spec=pltpu.PrefetchScalarGridSpec(
-            num_scalar_prefetch=1, grid=(slots,), in_specs=[own, own, arrived], out_specs=[out] * 4
+            num_scalar_prefetch=1,
+            grid=(2, slots),
+            in_specs=[own, own, arrived(0), arrived(2)],
+            out_specs=[acts, grads, acts, grads],
         ),
         out_shape=(shape,) * 4,
         compiler_params=pltpu.CompilerParams(vmem_limit_bytes=60 * 2**20),
         name="grams",
-    )(meta, first, moved, got)
+    )(meta, first, moved, got, got)
 
 
 def on_square(first_acts, first_grads, last_acts, last_grads, doc_lengths, block_owner):
@@ -362,7 +447,7 @@
 
     def branch(which):
         def run(meta, first, last):
-            got, moved, _ = exchange(which, sections, first, last)
+            got, moved, *_ = exchange(which, sections, first, last)
             return grams(meta, first, moved, got)
 
         return run

time: 176 us -> 185 us (1.051)
  the two profiles are of different devices: /device:TPU:16 before, /device:TPU:1 now
where the time goes in v3:
time: 185 us; the launch traced here: 184 us
  Pallas kernels  182 us (98%)
    pallas_call x1, Pallas kernels, exchange(): pl.pallas_call(functools.partial(exchange_kernel, most, sections), in_spe...  145 us
    pallas_call x1, Pallas kernels, grams(): pl.pallas_call(gram_kernel, grid_spec=pltpu.PrefetchScalarGridSpec(num_sc...  26.7 us
    pallas_call x1, Pallas kernels, arrange(): pl.pallas_call(arrange_kernel, grid_spec=pltpu.PrefetchScalarGridSpec(num...  10.9 us

profile of v3, /device:TPU:1, one launch (start us, length us, event | category | flops | bytes accessed | tf_op | source)
XLA Modules:
  0.0 184.2 jit_solution(13207922393508458293)
XLA Ops:
  0.6 10.9 %arrange.1 = (bf16[2,20,128,512]{3,2,1,0:T(8,128)(2,1)}, bf16[2,20,128,512]{3,2,1,0:T(8,128)(2,1)}, s32[4]{0:T(128)S(1)}) custom-call(s32[16]{0:T(128)} %owner_ref.1, s32[16]{0:T(128)} %bitcast.2, bf16[1,128,8192]{2,1,0:T(8,128)(2,1)} %fa_ref.1, bf16[1,128,8192]{2,1,0:T(8,128)(2,1)} %fg_ref.1, bf16[1,128,8192]{2,1,0:T(8,128)(2,1)} %la_ref.1, ...), custom_call_target="tpu_custom_call" | custom-call | tf_op jit(solution)/shard_map/arrange/pallas_call | solution.py:116
  11.5 0.6 slice.3
  12.8 171.3 %conditional.1 = ((f32[1,1,8,512,512]{4,3,2,1,0:T(8,128)}, f32[1,1,8,512,512]{4,3,2,1,0:T(8,128)}, f32[1,1,8,512,512]{4,3,2,1,0:T(8,128)}, f32[1,1,8,512,512]{4,3,2,1,0:T(8,128)})) conditional(s32[]{:T(128)} %bitcast.1, (bf16[2,20,128,512]{3,2,1,0:T(8,128)(2,1)}, bf16[2,20,128,512]{3,2,1,0:T(8,128)(2,1)}, ...), branch_computations={%region_0.0_spmd, %region_1.0_spmd, %region_2.0_spmd, %region_3.0_... | conditional | bytes 8 | solution.py:455
  12.8 144.6 %exchange_0.1 = (bf16[4,3,8,128,512]{4,3,2,1,0:T(8,128)(2,1)}, bf16[2,20,128,512]{3,2,1,0:T(8,128)(2,1)}, bf16[2,3,8,128,512]{4,3,2,1,0:T(8,128)(2,1)}, bf16[2,2...) custom-call(bf16[2,20,128,512]{3,2,1,0:T(8,128)(2,1)} %get-tuple-element.25.first.own_ref, ...), custom_call_target="tpu_custom_call" | custom-call | tf_op jit(solution)/shard_map/cond/branch_0_fun/exchange_0/pallas_call | solution.py:357
  157.3 26.7 %grams.4 = (f32[1,1,8,512,512]{4,3,2,1,0:T(8,128)}, f32[1,1,8,512,512]{4,3,2,1,0:T(8,128)}, f32[1,1,8,512,512]{4,3,2,1,0:T(8,128)}, f32[1,1,8,512,512]{4,3,2,1,0:T(8,128)}) custom-call(s32[4]{0:T(128)S(1)} %get-tuple-element.24.meta_ref, bf16[2,20,128,512]{3,2,1,0:T(8,128)(2,1)} %get-tuple-element.25.first.own_ref, ...), custom_call_target="tpu_custom_call" | custom-call | tf_op jit(solution)/shard_map/cond/branch_0_fun/grams/pallas_call | solution.py:429

commit v4 on v3

--- a/solution.py
+++ b/solution.py
@@ -34,100 +34,89 @@
     last_ref,
     meta_ref,
     weight,
-    staged,
-    sem,
+    held,
+    read_sem,
+    write_sem,
     place_of,
     count,
 ):
     docs = lengths_ref.shape[0]
-    blocks = owner_ref.shape[0]
-    rows = fa_ref.shape[1]
-    width = first_ref.shape[3]
-    step = pl.program_id(0)
-    steps = pl.num_programs(0)
-
-    @pl.when(step == 0)
-    def _():
-        row = lax.broadcasted_iota(jnp.int32, (rows, 128), 0)
-        length = jnp.ones((rows, 128), jnp.int32)
-        start = jnp.int32(0)
-        for d in range(docs):
-            size = lengths_ref[d]
-            length = jnp.where((row >= start) & (row < start + size), size, length)
-            start = start + size
-        weight[...] = jnp.sqrt((1.0 / length.astype(jnp.float32)) / jnp.float32(docs * GROUPS))
-        for g in range(GROUPS):
-            count[g] = 0
-        for b in range(blocks):
-            owner = owner_ref[b]
-            place_of[b] = count[owner]
-            count[owner] = count[owner] + 1
-        most = jnp.int32(0)
-        for g in range(1, GROUPS):
-            most = jnp.where(count[g] == 8, jnp.int32(g), most)
-        for b in range(blocks):
-            place = owner_ref[b] ^ most
-            place_of[b] = place_of[b] + jnp.where(place == 0, 0, 4 + 4 * place)
-        me = lax.axis_index("dp")
-        place = me ^ most
-        meta_ref[0] = jnp.where(place == 0, 0, 4 + 4 * place)
-        meta_ref[1] = count[me]
-        meta_ref[2] = lax.axis_index("section")
-        meta_ref[3] = most
-
-    def outgoing(at, slot):
-        copies = []
-        for k in range(2):
-            to = place_of[2 * at + k]
-            for n, ref in enumerate((first_ref, first_ref, last_ref, last_ref)):
-                copies.append(pltpu.make_async_copy(staged.at[slot, k, n], ref.at[n % 2, to], sem.at[slot, k, n]))
-        return copies
-
-    slot = lax.rem(step, 2)
-
-    @pl.when(step >= 2)
-    def _():
-        for one in outgoing(step - 2, slot):
-            one.wait()
-
-    row_weight = jnp.concatenate([weight[...]] * (width // 128), axis=1)
-    for k in range(2):
-        for n, ref in enumerate((fa_ref, fg_ref, la_ref, lg_ref)):
-            block = ref[0, :, k * width : (k + 1) * width].astype(jnp.float32)
-            staged[slot, k, n] = (block * row_weight).astype(jnp.bfloat16)
-    for one in outgoing(step, slot):
-        one.start()
-
-    @pl.when(step == steps - 1)
-    def _():
-        for one in outgoing(step - 1, 1 - slot):
-            one.wait()
-        for one in outgoing(step, slot):
-            one.wait()
+    blocks, _, rows, width = held.shape
+
+    def read(b, n):
+        ref = (fa_ref, fg_ref, la_ref, lg_ref)[n]
+        span = pl.ds(pl.multiple_of(b * width, width), width)
+        return pltpu.make_async_copy(ref.at[0, :, span], held.at[b, n], read_sem.at[b, n])
+
+    def write(b, n):
+        ref = (first_ref, first_ref, last_ref, last_ref)[n]
+        return pltpu.make_async_copy(held.at[b, n], ref.at[n % 2, place_of[b]], write_sem.at[b, n])
+
+    @pl.loop(0, blocks)
+    def _(b):
+        for n in range(4):
+            read(b, n).start()
+
+    row = lax.broadcasted_iota(jnp.int32, (rows, 128), 0)
+    length = jnp.ones((rows, 128), jnp.int32)
+    start = jnp.int32(0)
+    for d in range(docs):
+        size = lengths_ref[d]
+        length = jnp.where((row >= start) & (row < start + size), size, length)
+        start = start + size
+    weight[...] = jnp.sqrt((1.0 / length.astype(jnp.float32)) / jnp.float32(docs * GROUPS))
+    for g in range(GROUPS):
+        count[g] = 0
+    for b in range(blocks):
+        owner = owner_ref[b]
+        place_of[b] = count[owner]
+        count[owner] = count[owner] + 1
+    most = jnp.int32(0)
+    for g in range(1, GROUPS):
+        most = jnp.where(count[g] == 8, jnp.int32(g), most)
+    for b in range(blocks):
+        place = owner_ref[b] ^ most
+        place_of[b] = place_of[b] + jnp.where(place == 0, 0, 4 + 4 * place)
+    me = lax.axis_index("dp")
+    place = me ^ most
+    meta_ref[0] = jnp.where(place == 0, 0, 4 + 4 * place)
+    meta_ref[1] = count[me]
+    meta_ref[2] = lax.axis_index("section")
+    meta_ref[3] = most
+
+    @pl.loop(0, blocks)
+    def _(b):
+        row_weight = jnp.concatenate([weight[...]] * (width // 128), axis=1)
+        for n in range(4):
+            read(b, n).wait()
+            held[b, n] = (held[b, n].astype(jnp.float32) * row_weight).astype(jnp.bfloat16)
+            write(b, n).start()
+
+    @pl.loop(0, blocks)
+    def _(b):
+        for n in range(4):
+            write(b, n).wait()
 
 
 def arrange(owner, lengths, arrays):
     rows = arrays[0].shape[1]
     blocks = owner.shape[0]
     width = arrays[0].shape[2] // blocks
-    in_spec = pl.BlockSpec((1, rows, 2 * width), lambda i, owner, lengths: (0, 0, i))
     hbm = pl.BlockSpec(memory_space=pl.ANY)
+    smem = pl.BlockSpec(memory_space=pltpu.SMEM)
     shape = jax.ShapeDtypeStruct((2, 8 + 4 * (GROUPS - 1), rows, width), jnp.bfloat16)
     return pl.pallas_call(
         arrange_kernel,
-        grid_spec=pltpu.PrefetchScalarGridSpec(
-            num_scalar_prefetch=2,
-            grid=(blocks // 2,),
-            in_specs=[in_spec] * 4,
-            out_specs=[hbm, hbm, pl.BlockSpec(memory_space=pltpu.SMEM)],
-            scratch_shapes=[
-                pltpu.VMEM((rows, 128), jnp.float32),
-                pltpu.VMEM((2, 2, 4, rows, width), jnp.bfloat16),
-                pltpu.SemaphoreType.DMA((2, 2, 4)),
-                pltpu.SMEM((blocks,), jnp.int32),
-                pltpu.SMEM((GROUPS,), jnp.int32),
-            ],
-        ),
+        in_specs=[smem, smem] + [hbm] * 4,
+        out_specs=[hbm, hbm, smem],
+        scratch_shapes=[
+            pltpu.VMEM((rows, 128), jnp.float32),
+            pltpu.VMEM((blocks, 4, rows, width), jnp.bfloat16),
+            pltpu.SemaphoreType.DMA((blocks, 4)),
+            pltpu.SemaphoreType.DMA((blocks, 4)),
+            pltpu.SMEM((blocks,), jnp.int32),
+            pltpu.SMEM((GROUPS,), jnp.int32),
+        ],
         out_shape=(shape, shape, jax.ShapeDtypeStruct((4,), jnp.int32)),
         compiler_params=pltpu.CompilerParams(vmem_limit_bytes=60 * 2**20),
         name="arrange",
@@ -161,19 +150,24 @@
     leaving = jnp.where(core == 1, planes - 1 - plane, 0)
     entering = jnp.where((core == 0) & has_prev, planes - plane, 0)
 
-    def move(half):
-        return pltpu.make_async_remote_copy(
-            src_ref=last.at[half],
-            dst_ref=moved.at[half],
-            send_sem=move_send.at[half],
-            recv_sem=move_recv.at[half],
-            device_id={"section": section + 1},
-            device_id_type=MESH,
-        )
-
     def role(place):
         def peer(link):
             return {"dp": most ^ place ^ link}
+
+        others = [at for at in range(4) if at != place]
+
+        def move(half, at, quarter=None):
+            n = held_at(at) if quarter is None else held_at(at) // QUARTERS
+            span = pl.ds(base_of(at) + (0 if quarter is None else quarter * n), n)
+            index = 0 if quarter is None else quarter
+            return pltpu.make_async_remote_copy(
+                src_ref=last.at[half, span],
+                dst_ref=moved.at[half, span],
+                send_sem=move_send.at[half, at, index],
+                recv_sem=move_recv.at[half, at, index],
+                device_id={"section": section + 1},
+                device_id_type=MESH,
+            )
 
         def go_on(half, quarter):
             m = held_at(place) // QUARTERS
@@ -300,31 +294,40 @@
 
         pl.semaphore_wait(barrier, 2 + has_prev.astype(jnp.int32) + has_next.astype(jnp.int32))
 
-        @pl.when(has_next)
-        def _():
-            for half in range(2):
-                move(half).start()
-
-        for half in range(2):
-            whole(half).start()
-        each(0, leaving, lambda half, quarter: ahead(half, quarter).start())
-        for half in range(2):
-            whole(half).pass_on()
-        each(0, leaving, lambda half, quarter: ahead(half, quarter).pass_on())
-
         late_from = jnp.where(has_prev, entering, QUARTERS)
-
-        @pl.when(has_prev)
-        def _():
-            for half in range(2):
-                move(half).wait_recv()
-
-        each(late_from, QUARTERS, lambda half, quarter: late(half, quarter).start())
+        moving_from = jnp.where(has_next, leaving, QUARTERS)
+
+        def start_moves(half, quarter):
+            for at in others:
+                move(half, at, quarter).start()
+
+        def start_late(half, quarter):
+            for at in others:
+                move(half, at, quarter).wait_recv()
+            late(half, quarter).start()
 
         def send_on(half, quarter):
             ahead(half, quarter).wait_arrivals()
             go_on(half, quarter).start()
 
+        def wait_moves(half, quarter):
+            for at in others:
+                move(half, at, quarter).wait_send()
+
+        each(moving_from, QUARTERS, start_moves)
+        each(0, leaving, lambda half, quarter: ahead(half, quarter).start())
+        for half in range(2):
+            whole(half).start()
+
+        @pl.when(has_next)
+        def _():
+            for half in range(2):
+                move(half, place).start()
+
+        each(0, leaving, lambda half, quarter: ahead(half, quarter).pass_on())
+        for half in range(2):
+            whole(half).pass_on()
+        each(late_from, QUARTERS, start_late)
         each(0, leaving, send_on)
         each(late_from, QUARTERS, lambda half, quarter: late(half, quarter).pass_on())
 
@@ -332,16 +335,23 @@
             whole(half).wait_arrivals()
         each(late_from, QUARTERS, lambda half, quarter: late(half, quarter).wait_arrivals())
         each(0, entering, lambda half, quarter: go_on(half, quarter).wait_recv())
+
+        @pl.when(has_prev)
+        def _():
+            for half in range(2):
+                move(half, place).wait_recv()
+
         for half in range(2):
             whole(half).wait_sent()
         each(0, leaving, lambda half, quarter: ahead(half, quarter).wait_sent())
         each(0, leaving, lambda half, quarter: go_on(half, quarter).wait_send())
         each(late_from, QUARTERS, lambda half, quarter: late(half, quarter).wait_sent())
+        each(moving_from, QUARTERS, wait_moves)
 
         @pl.when(has_next)
         def _():
             for half in range(2):
-                move(half).wait_send()
+                move(half, place).wait_send()
 
     for place in range(4):
         pl.when(me == most ^ place)(functools.partial(role, place))
@@ -368,8 +378,8 @@
         scratch_shapes=[
             pltpu.SemaphoreType.DMA((2 + 4 * QUARTERS, 6)),
             pltpu.SemaphoreType.DMA((2 + 4 * QUARTERS, 6)),
-            pltpu.SemaphoreType.DMA((2,)),
-            pltpu.SemaphoreType.DMA((2,)),
+            pltpu.SemaphoreType.DMA((2, 4, QUARTERS)),
+            pltpu.SemaphoreType.DMA((2, 4, QUARTERS)),
             pltpu.SemaphoreType.DMA((2 * QUARTERS,)),
             pltpu.SemaphoreType.DMA((2 * QUARTERS,)),
         ],
@@ -380,33 +390,34 @@
     )(first, last)
 
 
-def gram_kernel(meta_ref, own_ref, own_last_ref, got_ref, got_last_ref, fa_ref, fg_ref, ca_ref, cg_ref):
-    side = pl.program_id(0)
-    filled = pl.program_id(1) < meta_ref[1]
-    crossed = filled & (meta_ref[2] > 0)
+def gram_kernel(meta_ref, own_ref, own_last_ref, got_ref, fa_ref, fg_ref, ca_ref, cg_ref):
+    filled = pl.program_id(0) < meta_ref[1]
+    has_prev = meta_ref[2] > 0
     contract = (((0,), (0,)), ((), ()))
 
-    def joined(own, got):
-        return jnp.concatenate([own[0, 0], got[0, 0, 0], got[0, 1, 0], got[0, 2, 0]], axis=0)
+    def joined(own, half, a):
+        return jnp.concatenate([own[half, 0], got_ref[a, 0, 0], got_ref[a, 1, 0], got_ref[a, 2, 0]], axis=0)
 
     for half, factor_ref, cross_ref in ((0, fa_ref, ca_ref), (1, fg_ref, cg_ref)):
 
-        @pl.when((side == half) & filled)
-        def _():
-            latter = joined(own_ref, got_ref)
+        @pl.when(filled & jnp.logical_not(has_prev))
+        def _():
+            latter = joined(own_ref, half, half)
             factor_ref[0, 0, 0] = lax.dot_general(latter, latter, contract, preferred_element_type=jnp.float32)
 
-        @pl.when((side == half) & crossed)
-        def _():
-            latter = joined(own_ref, got_ref)
-            former = joined(own_last_ref, got_last_ref)
-            cross_ref[0, 0, 0] = lax.dot_general(former, latter, contract, preferred_element_type=jnp.float32)
-
-        @pl.when((side == half) & jnp.logical_not(filled))
+        @pl.when(filled & has_prev)
+        def _():
+            latter = joined(own_ref, half, half)
+            both = jnp.concatenate([latter, joined(own_last_ref, half, 2 + half)], axis=1)
+            products = lax.dot_general(both, latter, contract, preferred_element_type=jnp.float32)
+            factor_ref[0, 0, 0] = products[: latter.shape[1]]
+            cross_ref[0, 0, 0] = products[latter.shape[1] :]
+
+        @pl.when(jnp.logical_not(filled))
         def _():
             factor_ref[...] = jnp.zeros_like(factor_ref)
 
-        @pl.when((side == half) & jnp.logical_not(crossed))
+        @pl.when(jnp.logical_not(filled & has_prev))
         def _():
             cross_ref[...] = jnp.zeros_like(cross_ref)
 
@@ -418,26 +429,19 @@
     def slot_of(i, meta):
         return jnp.minimum(i, jnp.maximum(meta[1] - 1, 0))
 
-    def arrived(skip):
-        return pl.BlockSpec((1, 3, 1, rows, width), lambda h, i, meta: (skip + h, 0, slot_of(i, meta), 0, 0))
-
-    own = pl.BlockSpec((1, 1, rows, width), lambda h, i, meta: (h, meta[0] + slot_of(i, meta), 0, 0))
-    block = (1, 1, 1, width, width)
-    acts = pl.BlockSpec(block, lambda h, i, meta: (0, 0, jnp.where(h == 0, i, slots - 1), 0, 0))
-    grads = pl.BlockSpec(block, lambda h, i, meta: (0, 0, jnp.where(h == 0, 0, i), 0, 0))
+    own = pl.BlockSpec((2, 1, rows, width), lambda i, meta: (0, meta[0] + slot_of(i, meta), 0, 0))
+    arrived = pl.BlockSpec((4, 3, 1, rows, width), lambda i, meta: (0, 0, slot_of(i, meta), 0, 0))
+    out = pl.BlockSpec((1, 1, 1, width, width), lambda i, meta: (0, 0, i, 0, 0))
     shape = jax.ShapeDtypeStruct((1, 1, slots, width, width), jnp.float32)
     return pl.pallas_call(
         gram_kernel,
         grid_spec=pltpu.PrefetchScalarGridSpec(
-            num_scalar_prefetch=1,
-            grid=(2, slots),
-            in_specs=[own, own, arrived(0), arrived(2)],
-            out_specs=[acts, grads, acts, grads],
+            num_scalar_prefetch=1, grid=(slots,), in_specs=[own, own, arrived], out_specs=[out] * 4
         ),
         out_shape=(shape,) * 4,
         compiler_params=pltpu.CompilerParams(vmem_limit_bytes=60 * 2**20),
         name="grams",
-    )(meta, first, moved, got, got)
+    )(meta, first, moved, got)
 
 
 def on_square(first_acts, first_grads, last_acts, last_grads, doc_lengths, block_owner):

time: 185 us -> 167 us (0.903)
  the two profiles are of different devices: /device:TPU:1 before, /device:TPU:13 now
where the time goes in v4:
time: 167 us
  Pallas kernels  165 us (99%)
    pallas_call x1, Pallas kernels, exchange(): pl.pallas_call(functools.partial(exchange_kernel, most, sections), in_spe...  134 us
    pallas_call x1, Pallas kernels, grams(): pl.pallas_call(gram_kernel, grid_spec=pltpu.PrefetchScalarGridSpec(num_sc...  21.7 us
    pallas_call x1, Pallas kernels, arrange(): pl.pallas_call(arrange_kernel, in_specs=[smem, smem] + [hbm] * 4, out_spe...  9.03 us

profile of v4, /device:TPU:13, one launch (start us, length us, event | category | flops | bytes accessed | tf_op | source)
XLA Modules:
  0.0 166.7 jit_solution(17881159800326305453)
XLA Ops:
  0.6 9.0 %arrange.1 = (bf16[2,20,128,512]{3,2,1,0:T(8,128)(2,1)}, bf16[2,20,128,512]{3,2,1,0:T(8,128)(2,1)}, s32[4]{0:T(128)S(1)}) custom-call(s32[16]{0:T(128)} %owner_ref.1, s32[16]{0:T(128)} %bitcast.2, bf16[1,128,8192]{2,1,0:T(8,128)(2,1)} %fa_ref.1, bf16[1,128,8192]{2,1,0:T(8,128)(2,1)} %fg_ref.1, bf16[1,128,8192]{2,1,0:T(8,128)(2,1)} %la_ref.1, ...), custom_call_target="tpu_custom_call" | custom-call | tf_op jit(solution)/shard_map/arrange/pallas_call | solution.py:108
  9.7 0.6 slice.3
  10.9 155.8 %conditional.1 = ((f32[1,1,8,512,512]{4,3,2,1,0:T(8,128)}, f32[1,1,8,512,512]{4,3,2,1,0:T(8,128)}, f32[1,1,8,512,512]{4,3,2,1,0:T(8,128)}, f32[1,1,8,512,512]{4,3,2,1,0:T(8,128)})) conditional(s32[]{:T(128)} %bitcast.1, (bf16[2,20,128,512]{3,2,1,0:T(8,128)(2,1)}, bf16[2,20,128,512]{3,2,1,0:T(8,128)(2,1)}, ...), branch_computations={%region_0.0_spmd, %region_1.0_spmd, %region_2.0_spmd, %region_3.0_... | conditional | bytes 8 | solution.py:459
  10.9 134.1 %exchange_2.1 = (bf16[4,3,8,128,512]{4,3,2,1,0:T(8,128)(2,1)}, bf16[2,20,128,512]{3,2,1,0:T(8,128)(2,1)}, bf16[2,3,8,128,512]{4,3,2,1,0:T(8,128)(2,1)}, bf16[2,2...) custom-call(bf16[2,20,128,512]{3,2,1,0:T(8,128)(2,1)} %get-tuple-element.35.first.own_ref, ...), custom_call_target="tpu_custom_call" | custom-call | tf_op jit(solution)/shard_map/cond/branch_2_fun/exchange_2/pallas_call | solution.py:367
  145.0 21.7 %grams.6 = (f32[1,1,8,512,512]{4,3,2,1,0:T(8,128)}, f32[1,1,8,512,512]{4,3,2,1,0:T(8,128)}, f32[1,1,8,512,512]{4,3,2,1,0:T(8,128)}, f32[1,1,8,512,512]{4,3,2,1,0:T(8,128)}) custom-call(s32[4]{0:T(128)S(1)} %get-tuple-element.34.meta_ref, bf16[2,20,128,512]{3,2,1,0:T(8,128)(2,1)} %get-tuple-element.35.first.own_ref, ...), custom_call_target="tpu_custom_call" | custom-call | tf_op jit(solution)/shard_map/cond/branch_2_fun/grams/pallas_call | solution.py:436

commit v5 on v4

--- a/solution.py
+++ b/solution.py
@@ -233,9 +233,11 @@
             def arrival(self, dst, received):
                 return self.copy(dst, dst, received, received, 1)
 
-            def start(self):
+            def start_hops(self):
                 for link in self.sends:
                     self.hop(link).start()
+
+            def start_direct(self):
                 for link in (1, 2):
                     self.direct(link).start()
 
@@ -304,7 +306,7 @@
         def start_late(half, quarter):
             for at in others:
                 move(half, at, quarter).wait_recv()
-            late(half, quarter).start()
+            late(half, quarter).start_hops()
 
         def send_on(half, quarter):
             ahead(half, quarter).wait_arrivals()
@@ -315,9 +317,12 @@
                 move(half, at, quarter).wait_send()
 
         each(moving_from, QUARTERS, start_moves)
-        each(0, leaving, lambda half, quarter: ahead(half, quarter).start())
+        each(0, leaving, lambda half, quarter: ahead(half, quarter).start_hops())
         for half in range(2):
-            whole(half).start()
+            whole(half).start_hops()
+        each(0, leaving, lambda half, quarter: ahead(half, quarter).start_direct())
+        for half in range(2):
+            whole(half).start_direct()
 
         @pl.when(has_next)
         def _():
@@ -328,6 +333,7 @@
         for half in range(2):
             whole(half).pass_on()
         each(late_from, QUARTERS, start_late)
+        each(late_from, QUARTERS, lambda half, quarter: late(half, quarter).start_direct())
         each(0, leaving, send_on)
         each(late_from, QUARTERS, lambda half, quarter: late(half, quarter).pass_on())
 

time: 167 us -> 168 us (level)
  the two profiles are of different devices: /device:TPU:13 before, /device:TPU:15 now
where the time goes in v5:
time: 168 us; the launch traced here: 170 us
  Pallas kernels  164 us (98%)
  loops' own time  4.18 us (2%)
    pallas_call x1, Pallas kernels, exchange(): pl.pallas_call(functools.partial(exchange_kernel, most, sections), in_spe...  133 us
    pallas_call x1, Pallas kernels, grams(): pl.pallas_call(gram_kernel, grid_spec=pltpu.PrefetchScalarGridSpec(num_sc...  21.7 us
    pallas_call x1, Pallas kernels, arrange(): pl.pallas_call(arrange_kernel, in_specs=[smem, smem] + [hbm] * 4, out_spe...  9.04 us
    another operation x1, loops' own time, on_square(): lax.switch(meta[3], [branch(which) for which in range(GROUPS)], meta, fir...  4.18 us

profile of v5, /device:TPU:15, one launch (start us, length us, event | category | flops | bytes accessed | tf_op | source)
XLA Modules:
  0.0 169.9 jit_solution(3764337519977318659)
XLA Ops:
  0.6 9.0 %arrange.1 = (bf16[2,20,128,512]{3,2,1,0:T(8,128)(2,1)}, bf16[2,20,128,512]{3,2,1,0:T(8,128)(2,1)}, s32[4]{0:T(128)S(1)}) custom-call(s32[16]{0:T(128)} %owner_ref.1, s32[16]{0:T(128)} %bitcast.2, bf16[1,128,8192]{2,1,0:T(8,128)(2,1)} %fa_ref.1, bf16[1,128,8192]{2,1,0:T(8,128)(2,1)} %fg_ref.1, bf16[1,128,8192]{2,1,0:T(8,128)(2,1)} %la_ref.1, ...), custom_call_target="tpu_custom_call" | custom-call | tf_op jit(solution)/shard_map/arrange/pallas_call | solution.py:108
  9.7 0.6 slice.3
  10.9 159.0 %conditional.1 = ((f32[1,1,8,512,512]{4,3,2,1,0:T(8,128)}, f32[1,1,8,512,512]{4,3,2,1,0:T(8,128)}, f32[1,1,8,512,512]{4,3,2,1,0:T(8,128)}, f32[1,1,8,512,512]{4,3,2,1,0:T(8,128)})) conditional(s32[]{:T(128)} %bitcast.1, (bf16[2,20,128,512]{3,2,1,0:T(8,128)(2,1)}, bf16[2,20,128,512]{3,2,1,0:T(8,128)(2,1)}, ...), branch_computations={%region_0.0_spmd, %region_1.0_spmd, %region_2.0_spmd, %region_3.0_... | conditional | bytes 8 | solution.py:465
  15.1 133.1 %exchange_3.1 = (bf16[4,3,8,128,512]{4,3,2,1,0:T(8,128)(2,1)}, bf16[2,20,128,512]{3,2,1,0:T(8,128)(2,1)}, bf16[2,3,8,128,512]{4,3,2,1,0:T(8,128)(2,1)}, bf16[2,2...) custom-call(bf16[2,20,128,512]{3,2,1,0:T(8,128)(2,1)} %get-tuple-element.40.first.own_ref, ...), custom_call_target="tpu_custom_call" | custom-call | tf_op jit(solution)/shard_map/cond/branch_3_fun/exchange_3/pallas_call | solution.py:373
  148.2 21.7 %grams.7 = (f32[1,1,8,512,512]{4,3,2,1,0:T(8,128)}, f32[1,1,8,512,512]{4,3,2,1,0:T(8,128)}, f32[1,1,8,512,512]{4,3,2,1,0:T(8,128)}, f32[1,1,8,512,512]{4,3,2,1,0:T(8,128)}) custom-call(s32[4]{0:T(128)S(1)} %get-tuple-element.39.meta_ref, bf16[2,20,128,512]{3,2,1,0:T(8,128)(2,1)} %get-tuple-element.40.first.own_ref, ...), custom_call_target="tpu_custom_call" | custom-call | tf_op jit(solution)/shard_map/cond/branch_3_fun/grams/pallas_call | solution.py:442
